TPU v7x, 128 devices: a whole 4x4x4 slice. The times are simulated.
128 devices in a mesh: dp: 8 (over x, core), table: 16 (over y, z).
Axes of the slice: x: 4, y: 4, z: 4, core: 2. Of those that a mesh axis runs over, the one named last changes fastest.
Arguments:
- grad_out: bfloat16 [32768, 4096], P(('dp', 'table')), may hold values from -6 to 6
- slot_weight: float32 [32768, 32], P(('dp', 'table')), may hold values from 0.05 to 1
- slot_pos: int32 [32768, 32], P(('dp', 'table')), may hold values from 0 to 511, as said below
- slot_rows: int32 [16, 128, 32], P('table'), may hold values from 0 to 1023
- values: float32 [16384, 4096], P('table', 'dp'), may hold values from -6 to 6
- first_moment: float32 [16384, 4096], P('table', 'dp'), may hold values from -4 to 4
- second_moment: float32 [16384, 4096], P('table', 'dp'), may hold values from 0.01 to 1
- row_steps: int32 [16384], P('table'), may hold values from 1 to 64
- queries: bfloat16 [32768, 2, 256], P(('dp', 'table')), may hold values from -6 to 6
- score_grad: bfloat16 [32768, 2, 4096], P(('dp', 'table')), may hold values from -0.03125 to 0.03125
Outputs:
- new_values: float32 [16384, 4096], P('table', 'dp')
- new_first: float32 [16384, 4096], P('table', 'dp')
- new_second: float32 [16384, 4096], P('table', 'dp')
- subkey_grad: bfloat16 [2, 4096, 256], replicated
Inputs may be any that keep to these rules, and one draw needn't show every extreme that they name: `slot_pos`: three owners drawn from the seed receive some three times the mean share of slots.
All inputs are finite; a program needn't handle non-finite values.
Results may differ from a plain program's by a relative error of at most 0.0058.
Values may be sent and summed in bfloat16 or wider, within the bound.
No kernel may reach another device: no remote copies, remote signals or barrier semaphores. Data moves between devices by JAX's collectives and lax.ppermute only.
A program may use at most 128 MiB of HBM per device.

v0:
```python
import jax
import jax.numpy as jnp
from jax import lax
from jax.sharding import PartitionSpec as P


def per_device(
    grad_out,
    slot_weight,
    slot_pos,
    slot_rows,
    values,
    first_moment,
    second_moment,
    row_steps,
    queries,
    score_grad,
):
    n_table = lax.axis_size("table")
    n_data = lax.axis_size("dp")
    width = grad_out.shape[1]
    columns = width // n_data
    cap_rows = slot_rows.shape[2]
    owned = values.shape[0]
    positions = jnp.arange(n_table * cap_rows, dtype=jnp.int32)
    hits = slot_pos[:, :, None] == positions[None, None, :]
    slot_mix = jnp.sum(jnp.where(hits, slot_weight[:, :, None], jnp.float32(0.0)), axis=1).astype(
        jnp.bfloat16
    )
    combined = lax.dot_general(
        slot_mix, grad_out, (((0,), (0,)), ((), ())), preferred_element_type=jnp.float32
    ).astype(jnp.bfloat16)
    blocks = combined.reshape(n_table, cap_rows, n_data, columns)
    partial_keys = jnp.einsum(
        "ths,thk->hsk", score_grad, queries, preferred_element_type=jnp.float32
    )
    subkey_out = lax.psum(partial_keys, ("dp", "table")).astype(jnp.bfloat16)
    own_rows = slot_rows[0]
    ordered = jnp.transpose(blocks, (2, 0, 1, 3)).reshape(n_data * n_table, cap_rows, columns)
    received = lax.all_to_all(ordered, ("dp", "table"), split_axis=0, concat_axis=0, tiled=True)
    arrived = received.reshape(-1, columns)
    row_index = own_rows.reshape(-1)
    selector = (jnp.arange(owned, dtype=jnp.int32)[:, None] == row_index[None, :]).astype(
        jnp.bfloat16
    )
    row_grad = jnp.dot(selector, arrived, preferred_element_type=jnp.float32)
    new_first = 0.9 * first_moment + 0.1 * row_grad
    new_second = 0.95 * second_moment + 0.05 * row_grad * row_grad
    steps = row_steps.astype(jnp.float32)[:, None]
    fix_first = 1.0 - jnp.exp(steps * jnp.log(jnp.float32(0.9)))
    fix_second = 1.0 - jnp.exp(steps * jnp.log(jnp.float32(0.95)))
    new_values = values - 0.1 * (new_first / fix_first) / (
        jnp.sqrt(new_second / fix_second) + 1e-08
    )
    return (new_values, new_first, new_second, subkey_out)


def solution(mesh):
    return jax.shard_map(
        per_device,
        mesh=mesh,
        in_specs=(
            P(("dp", "table"), None),
            P(("dp", "table"), None),
            P(("dp", "table"), None),
            P("table", None, None),
            P("table", "dp"),
            P("table", "dp"),
            P("table", "dp"),
            P("table"),
            P(("dp", "table"), None, None),
            P(("dp", "table"), None, None),
        ),
        out_specs=(P("table", "dp"), P("table", "dp"), P("table", "dp"), P()),
        check_vma=False,
    )
```

profile of v0, /device:TPU:1, one launch (start us, length us, event | category | flops | bytes accessed | tf_op | source)
XLA Modules:
  0.0 187.7 jit_solution(7461302966871747836)
XLA Ops:
  0.6 0.0 copy-start
  0.6 1.0 copy.26
  1.6 0.9 copy.25
  2.5 4.7 %select_reduce_fusion = bf16[256,512]{1,0:T(8,128)(2,1)S(1)} fusion(f32[256,32]{1,0:T(8,128)S(1)} %copy.26, s32[256,32]{1,0:T(8,128)S(1)} %copy.25), kind=kLoop, calls=%fused_computation | loop fusion | flops 12451840 | bytes 327680 | tf_op jit(solution)/shard_map/reduce_sum | solution.py:27
  7.2 0.0 copy-done
  7.2 1.3 convolution_convert_fusion
  8.5 2.2 %copy.30 = bf16[64,8,8,512]{3,2,1,0:T(8,128)(2,1)S(1)} copy(bf16[64,8,8,512]{3,1,2,0:T(8,128)(2,1)S(1)} %bitcast.11) | data formatting | bytes 8388608
  10.8 3.4 %copy.27 = bf16[16,32,8,512]{3,1,0,2:T(8,128)(2,1)} copy(bf16[16,32,8,512]{3,2,1,0:T(8,128)(2,1)S(1)} %bitcast.12) | data formatting | bytes 8388608 | tf_op jit(solution)/shard_map/reshape | solution.py:33
  14.1 0.0 copy-start.2
  14.1 0.0 copy-start.1
  14.1 12.0 %all-to-all-start = ((bf16[128,32,512]{2,1,0:T(8,128)(2,1)}), bf16[128,32,512]{2,1,0:T(8,128)(2,1)}, u32[]{:S(2)}, u32[]{:S(2)}) async-start(bf16[128,32,512]{2,1,0:T(8,128)(2,1)} %bitcast.10), calls=%async_computation | async-start | bytes 8388608 | tf_op jit(solution)/shard_map/all_to_all | solution.py:40
  26.1 0.0 copy-done.2
  26.1 0.1 copy.24
  26.2 0.1 eq.29
  26.3 0.0 copy-done.1
  26.3 0.0 copy-start.3
  26.3 10.6 %fusion.2 = f32[2,4096,256]{2,1,0:T(8,128)} fusion(bf16[256,2,4096]{2,1,0:T(2,128)(2,1)} %param.19, bf16[256,2,256]{2,1,0:T(2,128)(2,1)S(1)} %copy-done.1), kind=kOutput, calls=%fused_computation.6 | convolution fusion | flops 1073741824 | bytes 12845056 | tf_op jit(solution)/shard_map/ths,thk->hsk/dot_general | solution.py:34
  36.9 0.0 copy-done.3
  36.9 139.4 %all-reduce.1 = bf16[2,4096,256]{2,1,0:T(8,128)(2,1)} all-reduce(f32[2,4096,256]{2,1,0:T(8,128)} %fusion.2), channel_id=1, replica_groups=mesh['dp'=8,'table'=16] {'dp','table'}, use_global_device_ids=true, to_apply=%region_1.2 | all-reduce | flops 2097152 | bytes 12582912 | tf_op jit(solution)/shard_map/psum | solution.py:37
  176.3 0.0 all-to-all-done
  176.3 11.4 %divide_subtract_fusion = (f32[1024,512]{1,0:T(8,128)}, f32[1024,512]{1,0:T(8,128)}, f32[1024,512]{1,0:T(8,128)}) fusion(f32[1024,512]{1,0:T(8,128)} %param.14, f32[1024]{0:T(1024)S(1)} %get-tuple-element.8, f32[1024]{0:T(1024)S(1)} %get-tuple-element.7, f32[1024,512]{1,0:T(8,128)} %param.15, f32[1024,512]{1,0:T(8,128)} %param.16, ...), kind=kOutput, calls=%fused_computation.10 | convolution fusion | flops 4305977344 | bytes 16801792 | tf_op jit(solution)/shard_map/dot_general | solution.py:46
  (1 shorter events, 0.0 us)
Async XLA Ops:
  0.6 6.6 %copy-start = (bf16[256,4096]{1,0:T(8,128)(2,1)S(1)}, bf16[256,4096]{1,0:T(8,128)(2,1)}, u32[]{:S(2)}) copy-start(bf16[256,4096]{1,0:T(8,128)(2,1)} %param.10) | copy-start | bytes 6291460
  14.1 12.0 %copy-start.2 = (s32[1,128,32]{1,2,0:T(8,128)S(1)}, s32[1,128,32]{1,2,0:T(8,128)}, u32[]{:S(2)}) copy-start(s32[1,128,32]{1,2,0:T(8,128)} %param.13) | copy-start | bytes 49156
  14.1 12.2 %copy-start.1 = (bf16[256,2,256]{2,1,0:T(2,128)(2,1)S(1)}, bf16[256,2,256]{2,1,0:T(2,128)(2,1)}, u32[]{:S(2)}) copy-start(bf16[256,2,256]{2,1,0:T(2,128)(2,1)} %param.18) | copy-start | bytes 786436
  14.1 162.1 %all-to-all-start = ((bf16[128,32,512]{2,1,0:T(8,128)(2,1)}), bf16[128,32,512]{2,1,0:T(8,128)(2,1)}, u32[]{:S(2)}, u32[]{:S(2)}) async-start(bf16[128,32,512]{2,1,0:T(8,128)(2,1)} %bitcast.10), calls=%async_computation | async-start | bytes 8388608 | tf_op jit(solution)/shard_map/all_to_all | solution.py:40
  26.3 10.6 %copy-start.3 = (s32[1024]{0:T(1024)S(1)}, s32[1024]{0:T(1024)}, u32[]{:S(2)}) copy-start(s32[1024]{0:T(1024)} %param.17) | copy-start | bytes 12292
where the time goes:
time: 190 us; the launch traced here: 188 us
  blocking collectives  139 us (73%)
  matrix products  23.2 us (12%)
  starting transfers between devices  12 us (6%)
  local copies, waits for them, and re-layouts  7.68 us (4%)
  other arithmetic  4.7 us (2%)
    psum x1, blocking collectives, per_device(): subkey_out = lax.psum(partial_keys, ('dp', 'table')).astype(jnp.bfloat16)  139 us
    all_to_all x1, starting transfers between devices, per_device(): lax.all_to_all(ordered, ('dp', 'table'), split_axis=0, concat_axis=0, til...  12 us
    dot_general x1, matrix products, per_device(): row_grad = jnp.dot(selector, arrived, preferred_element_type=jnp.float32)  11.4 us
    dot_general x1, matrix products, per_device(): jnp.einsum('ths,thk->hsk', score_grad, queries, preferred_element_type=jn...  10.6 us
    reduce_sum x1, other arithmetic, per_device(): jnp.sum(jnp.where(hits, slot_weight[:, :, None], jnp.float32(0.0)), axis=1)  4.69 us
    unnamed x12, local copies, waits for them, and re-layouts  4.21 us
  transfers between devices with their start and end apart: 1, of which 0 were waited for; matrix products, arithmetic and copies ran while one was open for 6% of the time, Pallas kernels for 0%

commit v1 on v0

v1 whole, which is shorter than its diff:
```python
import jax
import jax.numpy as jnp
from jax import lax
from jax.experimental import pallas as pl
from jax.experimental.pallas import tpu as pltpu
from jax.sharding import PartitionSpec as P

AXES = ("dp", "table")
ROLES = (("x", "y", "z"), ("z", "x", "y"))
BF = jnp.bfloat16
F32 = jnp.float32


def coords(i):
    dp, table = i // 16, i % 16
    return {"x": dp // 2, "core": dp % 2, "y": table // 4, "z": table % 4}


def index_of(c):
    return (c["x"] * 2 + c["core"]) * 16 + c["y"] * 4 + c["z"]


def ring(role, shift):
    pairs = []
    for i in range(128):
        c = coords(i)
        axis = ROLES[c["core"]][role]
        c[axis] = (c[axis] + shift) % 4
        pairs.append((i, index_of(c)))
    return pairs


SWAP = [(i, i ^ 16) for i in range(128)]


def send(value, pairs):
    return lax.ppermute(value, AXES, pairs)


def combine_kernel(pos_ref, weight_ref, grad_ref, out_ref, mix_ref):
    slots, tokens = pos_ref.shape
    rows = mix_ref.shape[0]
    step = 64

    @pl.when(pl.program_id(0) == 0)
    def _():
        def block(b, carry):
            base = pl.multiple_of(b * step, step)
            place = lax.broadcasted_iota(jnp.int32, (step, tokens), 0) + base
            total = jnp.zeros((step, tokens), F32)
            for j in range(slots):
                hit = pos_ref[j : j + 1, :] == place
                total = total + jnp.where(hit, weight_ref[j : j + 1, :], 0.0)
            mix_ref[pl.ds(base, step), :] = total.astype(BF)
            return carry

        lax.fori_loop(0, rows // step, block, 0)

    product = jnp.dot(mix_ref[...], grad_ref[...], preferred_element_type=F32)
    out_ref[...] = product.astype(BF).reshape(out_ref.shape)


def combine(slot_pos, slot_weight, grad_out, n_data, n_table, cap):
    tokens, width = grad_out.shape
    slots = slot_pos.shape[1]
    columns = width // n_data
    return pl.pallas_call(
        combine_kernel,
        grid=(n_data,),
        in_specs=[
            pl.BlockSpec((slots, tokens), lambda i: (0, 0)),
            pl.BlockSpec((slots, tokens), lambda i: (0, 0)),
            pl.BlockSpec((tokens, columns), lambda i: (0, i)),
        ],
        out_specs=pl.BlockSpec((n_table, cap, columns), lambda i: (i, 0, 0)),
        out_shape=jax.ShapeDtypeStruct((n_data * n_table, cap, columns), BF),
        scratch_shapes=[pltpu.VMEM((n_table * cap, tokens), BF)],
        compiler_params=pltpu.CompilerParams(vmem_limit_bytes=32 << 20),
        name="combine",
    )(slot_pos.T, slot_weight.T, grad_out)


def partials_kernel(place_ref, score_ref, query_ref, own_ref, other_ref):
    score = score_ref[...].reshape(-1, score_ref.shape[2])
    query = query_ref[...].reshape(-1, query_ref.shape[2]).astype(F32)
    parity = lax.broadcasted_iota(jnp.int32, query.shape, 0) & 1
    own = jnp.where(parity == place_ref[0], query, 0.0)
    both = jnp.concatenate([own, query - own], axis=1).astype(BF)
    product = lax.dot_general(
        score, both, (((0,), (0,)), ((), ())), preferred_element_type=F32
    ).astype(BF)
    for j in range(4):
        rows = product[j * 256 : (j + 1) * 256]
        own_ref[0, (j - place_ref[2] + 4) % 4] = rows[:, :256]
        other_ref[0, (j - place_ref[5] + 4) % 4] = rows[:, 256:]


def partials(places, score, query):
    tokens, halves, keys = score.shape
    depth = query.shape[2]
    shape = jax.ShapeDtypeStruct((4, 4, 256, depth), BF)
    return pl.pallas_call(
        partials_kernel,
        grid_spec=pltpu.PrefetchScalarGridSpec(
            num_scalar_prefetch=1,
            grid=(4,),
            in_specs=[
                pl.BlockSpec((tokens, halves, keys // 4), lambda i, p: (0, 0, i)),
                pl.BlockSpec((tokens, halves, depth), lambda i, p: (0, 0, 0)),
            ],
            out_specs=[
                pl.BlockSpec((1, 4, 256, depth), lambda i, p: ((i - p[1] + 4) % 4, 0, 0, 0)),
                pl.BlockSpec((1, 4, 256, depth), lambda i, p: ((i - p[4] + 4) % 4, 0, 0, 0)),
            ],
        ),
        out_shape=[shape] * 2,
        compiler_params=pltpu.CompilerParams(vmem_limit_bytes=32 << 20),
        name="partials",
    )(places, score, query)


def merge_kernel(own_ref, got_ref, *out_refs):
    for r, out_ref in enumerate(out_refs):
        out_ref[...] = (own_ref[r].astype(F32) + got_ref[r].astype(F32)).astype(BF)


def merge(own, got):
    return pl.pallas_call(
        merge_kernel,
        out_shape=[jax.ShapeDtypeStruct(own.shape[1:], BF)] * 4,
        compiler_params=pltpu.CompilerParams(vmem_limit_bytes=32 << 20),
        name="merge",
    )(own, got)


def sum_kernel(a_ref, b_ref, c_ref, d_ref, *out_refs):
    for r, out_ref in enumerate(out_refs):
        near = a_ref[r].astype(F32) + c_ref[r].astype(F32)
        far = b_ref[r].astype(F32) + d_ref[r].astype(F32)
        out_ref[...] = (near + far).astype(BF)


def sum_chunks(chunks):
    shape = jax.ShapeDtypeStruct(chunks[0].shape[1:], BF)
    return pl.pallas_call(
        sum_kernel,
        out_shape=[shape] * 4,
        compiler_params=pltpu.CompilerParams(vmem_limit_bytes=32 << 20),
        name="sum_chunks",
    )(*chunks)


def place_kernel(place_ref, *refs):
    blocks, (out_ref, held, sem_in, sem_out) = refs[:8], refs[8:]
    loads = [pltpu.make_async_copy(blocks[k], held.at[k], sem_in.at[k]) for k in range(8)]
    for load in loads:
        load.start()
    stores = []
    for k in range(8):
        half, rb = k // 4, k % 4
        loads[k].wait()
        for ra in range(4):
            a = (place_ref[3 * half + 1] + ra) % 4
            b = (place_ref[3 * half + 2] + rb) % 4
            start = pl.multiple_of((a * 4 + b) * 256, 256)
            store = pltpu.make_async_copy(
                held.at[k, ra],
                out_ref.at[place_ref[3 * half], pl.ds(start, 256)],
                sem_out.at[k * 4 + ra],
            )
            store.start()
            stores.append(store)
    for store in stores:
        store.wait()


def place_blocks(places, buffers):
    return pl.pallas_call(
        place_kernel,
        in_specs=[pl.BlockSpec(memory_space=pltpu.SMEM)] + [pl.BlockSpec(memory_space=pl.ANY)] * 8,
        out_specs=pl.BlockSpec(memory_space=pl.ANY),
        out_shape=jax.ShapeDtypeStruct((2, 4096, 256), BF),
        scratch_shapes=[
            pltpu.VMEM((8, *buffers[0].shape), BF),
            pltpu.SemaphoreType.DMA((8,)),
            pltpu.SemaphoreType.DMA((32,)),
        ],
        compiler_params=pltpu.CompilerParams(vmem_limit_bytes=16 << 20),
        name="place_blocks",
    )(places, *buffers)


def adam_kernel(index_ref, steps_ref, arrived_ref, v_ref, m_ref, s_ref, nv_ref, nm_ref, ns_ref):
    rows, columns = v_ref.shape
    slots = index_ref.shape[1]
    base = pl.program_id(0) * rows
    place = lax.broadcasted_iota(jnp.int32, (rows, slots), 0) + base
    selector = jnp.where(index_ref[...] == place, 1.0, 0.0).astype(BF)
    grad = jnp.dot(selector, arrived_ref[...], preferred_element_type=F32)
    steps = steps_ref[0].astype(F32)
    first = 1.0 / (1.0 - jnp.exp(steps * jnp.log(jnp.float32(0.9))))
    second = 1.0 / (1.0 - jnp.exp(steps * jnp.log(jnp.float32(0.95))))
    first = jnp.broadcast_to(first, (128, rows)).T[:, :1]
    second = jnp.broadcast_to(second, (128, rows)).T[:, :1]
    new_first = 0.9 * m_ref[...] + 0.1 * grad
    new_second = 0.95 * s_ref[...] + 0.05 * grad * grad
    nm_ref[...] = new_first
    ns_ref[...] = new_second
    nv_ref[...] = v_ref[...] - 0.1 * (new_first * first) / (jnp.sqrt(new_second * second) + 1e-08)


def adam(index, steps, arrived, values, first_moment, second_moment):
    owned, columns = values.shape
    rows = 256
    slots = index.shape[1]
    block = pl.BlockSpec((rows, columns), lambda i: (i, 0))
    shape = jax.ShapeDtypeStruct(values.shape, F32)
    return pl.pallas_call(
        adam_kernel,
        grid=(owned // rows,),
        in_specs=[
            pl.BlockSpec((1, slots), lambda i: (0, 0)),
            pl.BlockSpec((1, 1, rows), lambda i: (i, 0, 0)),
            pl.BlockSpec((slots, columns), lambda i: (0, 0)),
            block,
            block,
            block,
        ],
        out_specs=[block] * 3,
        out_shape=[shape] * 3,
        compiler_params=pltpu.CompilerParams(vmem_limit_bytes=40 << 20),
        name="adam",
    )(index, steps, arrived, values, first_moment, second_moment)


def places_of():
    dp, table = lax.axis_index("dp"), lax.axis_index("table")
    at = {"x": dp // 2, "y": table // 4, "z": table % 4}
    core = dp % 2
    rows = []
    for c in (core, 1 - core):
        a = jnp.where(c == 0, at[ROLES[0][0]], at[ROLES[1][0]])
        b = jnp.where(c == 0, at[ROLES[0][1]], at[ROLES[1][1]])
        rows += [c, a, b]
    return jnp.stack(rows).astype(jnp.int32)


def per_device(
    grad_out,
    slot_weight,
    slot_pos,
    slot_rows,
    values,
    first_moment,
    second_moment,
    row_steps,
    queries,
    score_grad,
):
    n_table = lax.axis_size("table")
    n_data = lax.axis_size("dp")
    cap = slot_rows.shape[2]
    columns = values.shape[1]
    places = places_of()

    own, other = partials(places, score_grad, queries)
    got = send(other, SWAP)
    ordered = combine(slot_pos, slot_weight, grad_out, n_data, n_table, cap)
    chunks = merge(own, got)
    ordered, chunks = lax.optimization_barrier((ordered, chunks))
    chunks = [chunks[0]] + [send(chunks[r], ring(0, r)) for r in (1, 2, 3)]
    arrived = lax.all_to_all(ordered, AXES, split_axis=0, concat_axis=0, tiled=True)
    parts = sum_chunks(chunks)
    parts = [parts[0]] + [send(parts[r], ring(1, r)) for r in (1, 2, 3)]
    near = parts[0].astype(F32) + parts[2].astype(F32)
    total = (near + (parts[1].astype(F32) + parts[3].astype(F32))).astype(BF)
    around = [send(total, ring(2, r)) for r in (1, 2, 3)]
    near = total.astype(F32) + around[1].astype(F32)
    final = (near + (around[0].astype(F32) + around[2].astype(F32))).astype(BF)
    mine = jnp.stack([final] + [send(final, ring(0, -r)) for r in (1, 2, 3)])
    buffers = [mine] + [send(mine, ring(1, -r)) for r in (1, 2, 3)]
    buffers += [send(b, SWAP) for b in buffers]
    outs = adam(
        slot_rows.reshape(1, -1),
        row_steps.reshape(-1, 1, 256),
        arrived.reshape(-1, columns),
        values,
        first_moment,
        second_moment,
    )
    places, outs = lax.optimization_barrier((places, outs))
    subkey_out = place_blocks(places, buffers)
    return (*outs, subkey_out)


def solution(mesh):
    return jax.shard_map(
        per_device,
        mesh=mesh,
        in_specs=(
            P(("dp", "table"), None),
            P(("dp", "table"), None),
            P(("dp", "table"), None),
            P("table", None, None),
            P("table", "dp"),
            P("table", "dp"),
            P("table", "dp"),
            P("table"),
            P(("dp", "table"), None, None),
            P(("dp", "table"), None, None),
        ),
        out_specs=(P("table", "dp"), P("table", "dp"), P("table", "dp"), P()),
        check_vma=False,
    )
```

time: 190 us -> 156 us (0.82)
  blocking collectives: 139 us -> 0 us
  waiting for transfers between devices: 0.01 us -> 70.4 us
  starting transfers between devices: 12 us -> 50.3 us
  Pallas kernels: 0 us -> 23.5 us
  matrix products: 23.2 us -> 0 us
  other arithmetic: 4.7 us -> 0.2 us
  local copies, waits for them, and re-layouts: 7.68 us -> 10.2 us
    psum x1 -> x0, blocking collectives: 139 us -> none  [per_device(): subkey_out = lax.psum(partial_keys, ('dp', 'table')).astype(jnp.bfloat16)]
    ppermute x0 -> x20, waiting for transfers between devices: none -> 70.4 us  [send(): return lax.ppermute(value, AXES, pairs)]
    ppermute x0 -> x20, starting transfers between devices: none -> 39.6 us  [send(): return lax.ppermute(value, AXES, pairs)]
    pallas_call x0 -> x6, Pallas kernels: none -> 23.5 us  [the longest x1 9.55 us: adam(): pl.pallas_call(adam_kernel, grid=(owned // rows,), in_specs=[pl.BlockSpec...]
    dot_general x3 -> x0, matrix products: 23.2 us -> none  [the longest x1 11.4 us: per_device(): row_grad = jnp.dot(selector, arrived, preferred_element_type=jnp.float32)]
    unnamed x12 -> x27, local copies, waits for them, and re-layouts: 4.21 us -> 10 us
    reduce_sum x1 -> x0, other arithmetic: 4.69 us -> none  [per_device(): jnp.sum(jnp.where(hits, slot_weight[:, :, None], jnp.float32(0.0)), axis=1)]
    reshape x1, local copies, waits for them, and re-layouts: 3.39 us -> 0.1 us  [per_device(): slot_rows.reshape(1, -1)]
  transfers between devices with their start and end apart: 1 -> 21, of which waited for: 0 -> 8; matrix products, arithmetic and copies ran while one was open for 6% -> 0% of each run, Pallas kernels for 0% -> 9%
where the time goes in v1:
time: 156 us; the launch traced here: 155 us
  waiting for transfers between devices  70.4 us (45%)
  starting transfers between devices  50.3 us (32%)
  Pallas kernels  23.5 us (15%)
  local copies, waits for them, and re-layouts  10.2 us (7%)
    ppermute x20, waiting for transfers between devices, send(): return lax.ppermute(value, AXES, pairs)  70.4 us
    ppermute x20, starting transfers between devices, send(): return lax.ppermute(value, AXES, pairs)  39.6 us
    all_to_all x1, starting transfers between devices, per_device(): lax.all_to_all(ordered, AXES, split_axis=0, concat_axis=0, tiled=True)  10.7 us
    unnamed x27, local copies, waits for them, and re-layouts  10 us
    pallas_call x1, Pallas kernels, adam(): pl.pallas_call(adam_kernel, grid=(owned // rows,), in_specs=[pl.BlockSpec...  9.55 us
    pallas_call x1, Pallas kernels, partials(): pl.pallas_call(partials_kernel, grid_spec=pltpu.PrefetchScalarGridSpec(nu...  4.73 us
    pallas_call x1, Pallas kernels, combine(): pl.pallas_call(combine_kernel, grid=(n_data,), in_specs=[pl.BlockSpec((sl...  4.52 us
    pallas_call x1, Pallas kernels, place_blocks(): pl.pallas_call(place_kernel, in_specs=[pl.BlockSpec(memory_space=pltpu.SM...  4.01 us
  transfers between devices with their start and end apart: 21, of which 8 were waited for; matrix products, arithmetic and copies ran while one was open for 0% of the time, Pallas kernels for 9%

profile of v1, /device:TPU:1, one launch (start us, length us, event | category | flops | bytes accessed | tf_op | source)
XLA Modules:
  0.0 155.5 jit_solution(1214092553897190581)
XLA Ops:
  0.8 2.2 %copy-done.1 = bf16[256,2,4096]{2,1,0:T(2,128)(2,1)S(1)} copy-done((bf16[256,2,4096]{2,1,0:T(2,128)(2,1)S(1)}, bf16[256,2,4096]{2,1,0:T(2,128)(2,1)}, u32[]{:S(2)}) %copy-start.1) | copy-done | bytes 4194328
  3.0 0.9 copy-done.6
  3.9 4.7 %partials.1 = (bf16[4,4,256,256]{3,2,1,0:T(8,128)(2,1)S(1)}, bf16[4,4,256,256]{3,2,1,0:T(8,128)(2,1)S(1)}) custom-call(s32[6]{0:T(128)S(1)} %stack.42.place_ref, bf16[256,2,4096]{2,1,0:T(2,128)(2,1)S(1)} %copy-done.1, bf16[256,2,256]{2,1,0:T(2,128)(2,1)S(1)} %copy-done.6), custom_call_target="tpu_custom_call" | custom-call | tf_op jit(solution)/shard_map/partials/pallas_call | solution.py:102
  8.6 1.5 collective-permute-start
  10.2 4.5 %combine.1 = bf16[128,32,512]{2,1,0:T(8,128)(2,1)S(1)} custom-call(s32[32,256]{1,0:T(8,128)S(1)} %bitcast.14, f32[32,256]{1,0:T(8,128)S(1)} %bitcast.15, bf16[256,4096]{1,0:T(8,128)(2,1)S(1)} %copy-done.2), custom_call_target="tpu_custom_call" | custom-call | tf_op jit(solution)/shard_map/combine/pallas_call | solution.py:67
  14.7 2.0 %copy-done = bf16[128,32,512]{2,1,0:T(8,128)(2,1)} copy-done((bf16[128,32,512]{2,1,0:T(8,128)(2,1)}, bf16[128,32,512]{2,1,0:T(8,128)(2,1)S(1)}, u32[]{:S(2)}) %copy-start) | copy-done | bytes 4194328
  18.0 0.8 copy-done.11
  18.8 10.7 %all-to-all-start = ((bf16[128,32,512]{2,1,0:T(8,128)(2,1)}), bf16[128,32,512]{2,1,0:T(8,128)(2,1)}, u32[]{:S(2)}, u32[]{:S(2)}) async-start(bf16[128,32,512]{2,1,0:T(8,128)(2,1)} %copy-done), calls=%async_computation | async-start | bytes 8388608 | tf_op jit(solution)/shard_map/all_to_all | solution.py:272
  29.5 1.6 %collective-permute-start.1 = (bf16[4,256,256]{2,1,0:T(8,128)(2,1)}, bf16[4,256,256]{2,1,0:T(8,128)(2,1)S(1)}, u32[]{:S(2)}, u32[]{:S(2)}) collective-permute-start(bf16[4,256,256]{2,1,0:T(8,128)(2,1)} %copy-done.11), channel_id=1, source_target_pairs={{0,32},{1,33},{2,34},{3,35},{4,36},{5,37},{6,38},{7,39},{8,40},{9,... | collective-permute-start | bytes 1572872 | tf_op jit(solution)/shard_map/ppermute | solution.py:37
  31.0 2.9 %collective-permute-start.2 = (bf16[4,256,256]{2,1,0:T(8,128)(2,1)}, bf16[4,256,256]{2,1,0:T(8,128)(2,1)S(1)}, u32[]{:S(2)}, u32[]{:S(2)}) collective-permute-start(bf16[4,256,256]{2,1,0:T(8,128)(2,1)} %copy-done.10), channel_id=1, source_target_pairs={{0,64},{1,65},{2,66},{3,67},{4,68},{5,69},{6,70},{7,71},{8,72},{9,... | collective-permute-start | bytes 1572872 | tf_op jit(solution)/shard_map/ppermute | solution.py:37
  34.0 0.9 collective-permute-start.3
  34.9 48.7 %collective-permute-done.1.b_ref = bf16[4,256,256]{2,1,0:T(8,128)(2,1)S(1)} collective-permute-done((bf16[4,256,256]{2,1,0:T(8,128)(2,1)}, bf16[4,256,256]{2,1,0:T(8,128)(2,1)S(1)}, u32[]{:S(2)}, u32[]{:S(2)}) %collective-permute-start.1) | collective-permute-done | bytes 524320 | tf_op jit(solution)/shard_map/ppermute | solution.py:37
  83.6 7.5 %collective-permute-done.2.c_ref = bf16[4,256,256]{2,1,0:T(8,128)(2,1)S(1)} collective-permute-done((bf16[4,256,256]{2,1,0:T(8,128)(2,1)}, bf16[4,256,256]{2,1,0:T(8,128)(2,1)S(1)}, u32[]{:S(2)}, u32[]{:S(2)}) %collective-permute-start.2) | collective-permute-done | bytes 524320 | tf_op jit(solution)/shard_map/ppermute | solution.py:37
  91.3 2.5 %collective-permute-start.6 = (bf16[256,256]{1,0:T(8,128)(2,1)S(1)}, bf16[256,256]{1,0:T(8,128)(2,1)S(1)}, u32[]{:S(2)}, u32[]{:S(2)}) collective-permute-start(bf16[256,256]{1,0:T(8,128)(2,1)S(1)} %get-tuple-element.47), channel_id=1, source_target_pairs={{0,12},{1,13},{2,14},{3,15},{4,0},{5,1},{6,2},{7,3},{8,4},{9,5},{1... | collective-permute-start | bytes 393224 | tf_op jit(solution)/shard_map/ppermute | solution.py:37
  93.8 1.3 collective-permute-start.4
  95.8 4.5 %collective-permute-done.5 = bf16[256,256]{1,0:T(8,128)(2,1)S(1)} collective-permute-done((bf16[256,256]{1,0:T(8,128)(2,1)S(1)}, bf16[256,256]{1,0:T(8,128)(2,1)S(1)}, u32[]{:S(2)}, u32[]{:S(2)}) %collective-permute-start.5) | collective-permute-done | bytes 131104 | tf_op jit(solution)/shard_map/ppermute | solution.py:37
  100.3 1.6 %collective-permute-start.9 = (bf16[256,256]{1,0:T(8,128)(2,1)S(1)}, bf16[256,256]{1,0:T(8,128)(2,1)S(1)}, u32[]{:S(2)}, u32[]{:S(2)}) collective-permute-start(bf16[256,256]{1,0:T(8,128)(2,1)S(1)} %add_convert_fusion.1), channel_id=1, source_target_pairs={{0,3},{1,0},{2,1},{3,2},{4,7},{5,4},{6,5},{7,6},{8,11},{9,8},{10,9... | collective-permute-start | bytes 393224 | tf_op jit(solution)/shard_map/ppermute | solution.py:37
  102.0 1.6 %collective-permute-start.7 = (bf16[256,256]{1,0:T(8,128)(2,1)S(1)}, bf16[256,256]{1,0:T(8,128)(2,1)S(1)}, u32[]{:S(2)}, u32[]{:S(2)}) collective-permute-start(bf16[256,256]{1,0:T(8,128)(2,1)S(1)} %add_convert_fusion.1), channel_id=1, source_target_pairs={{0,2},{1,3},{2,0},{3,1},{4,6},{5,7},{6,4},{7,5},{8,10},{9,11},{10,... | collective-permute-start | bytes 393224 | tf_op jit(solution)/shard_map/ppermute | solution.py:37
  103.5 1.0 collective-permute-done.9
  104.5 4.2 %collective-permute-done.8 = bf16[256,256]{1,0:T(8,128)(2,1)S(1)} collective-permute-done((bf16[256,256]{1,0:T(8,128)(2,1)S(1)}, bf16[256,256]{1,0:T(8,128)(2,1)S(1)}, u32[]{:S(2)}, u32[]{:S(2)}) %collective-permute-start.8) | collective-permute-done | bytes 131104 | tf_op jit(solution)/shard_map/ppermute | solution.py:37
  108.8 1.5 collective-permute-start.11
  110.3 2.0 %collective-permute-start.10 = (bf16[256,256]{1,0:T(8,128)(2,1)S(1)}, bf16[256,256]{1,0:T(8,128)(2,1)S(1)}, u32[]{:S(2)}, u32[]{:S(2)}) collective-permute-start(bf16[256,256]{1,0:T(8,128)(2,1)S(1)} %add_convert_fusion), channel_id=1, source_target_pairs={{0,96},{1,97},{2,98},{3,99},{4,100},{5,101},{6,102},{7,103},{8,104... | collective-permute-start | bytes 393224 | tf_op jit(solution)/shard_map/ppermute | solution.py:37
  112.3 3.3 %collective-permute-done.12 = bf16[256,256]{1,0:T(8,128)(2,1)S(1)} collective-permute-done((bf16[256,256]{1,0:T(8,128)(2,1)S(1)}, bf16[256,256]{1,0:T(8,128)(2,1)S(1)}, u32[]{:S(2)}, u32[]{:S(2)}) %collective-permute-start.12) | collective-permute-done | bytes 131104 | tf_op jit(solution)/shard_map/ppermute | solution.py:37
  116.2 1.3 collective-permute-start.13
  118.2 6.6 %collective-permute-start.16 = (bf16[4,256,256]{2,1,0:T(8,128)(2,1)S(1)}, bf16[4,256,256]{2,1,0:T(8,128)(2,1)}, u32[]{:S(2)}, u32[]{:S(2)}) collective-permute-start(bf16[4,256,256]{2,1,0:T(8,128)(2,1)S(1)} %pad_maximum_fusion.refs_0_), channel_id=1, source_target_pairs={{0,16},{1,17},{2,18},{3,19},{4,20},{5,21},{6,22},{7,23},{8,24},{9,... | collective-permute-start | bytes 1572872 | tf_op jit(solution)/shard_map/ppermute | solution.py:37
  124.9 5.1 %collective-permute-start.17 = (bf16[4,256,256]{2,1,0:T(8,128)(2,1)S(1)}, bf16[4,256,256]{2,1,0:T(8,128)(2,1)}, u32[]{:S(2)}, u32[]{:S(2)}) collective-permute-start(bf16[4,256,256]{2,1,0:T(8,128)(2,1)S(1)} %collective-permute-done.13.refs_1_), channel_id=1, source_target_pairs={{0,16},{1,17},{2,18},{3,19},{4,20},{5,21},{6,22},{7,23},{8,24},{9,... | collective-permute-start | bytes 1572872 | tf_op jit(solution)/shard_map/ppermute | solution.py:37
  129.9 3.0 %collective-permute-start.18 = (bf16[4,256,256]{2,1,0:T(8,128)(2,1)}, bf16[4,256,256]{2,1,0:T(8,128)(2,1)}, u32[]{:S(2)}, u32[]{:S(2)}) collective-permute-start(bf16[4,256,256]{2,1,0:T(8,128)(2,1)} %collective-permute-done.14.refs_2_), channel_id=1, source_target_pairs={{0,16},{1,17},{2,18},{3,19},{4,20},{5,21},{6,22},{7,23},{8,24},{9,... | collective-permute-start | bytes 1572872 | tf_op jit(solution)/shard_map/ppermute | solution.py:37
  132.9 5.5 %collective-permute-start.19 = (bf16[4,256,256]{2,1,0:T(8,128)(2,1)}, bf16[4,256,256]{2,1,0:T(8,128)(2,1)}, u32[]{:S(2)}, u32[]{:S(2)}) collective-permute-start(bf16[4,256,256]{2,1,0:T(8,128)(2,1)} %collective-permute-done.15.refs_3_), channel_id=1, source_target_pairs={{0,16},{1,17},{2,18},{3,19},{4,20},{5,21},{6,22},{7,23},{8,24},{9,... | collective-permute-start | bytes 1572872 | tf_op jit(solution)/shard_map/ppermute | solution.py:37
  138.7 1.6 %copy-done.4 = f32[1024,512]{1,0:T(8,128)S(1)} copy-done((f32[1024,512]{1,0:T(8,128)S(1)}, f32[1024,512]{1,0:T(8,128)}, u32[]{:S(2)}) %copy-start.4) | copy-done | bytes 2097176
  140.3 1.6 %copy-done.5 = f32[1024,512]{1,0:T(8,128)S(1)} copy-done((f32[1024,512]{1,0:T(8,128)S(1)}, f32[1024,512]{1,0:T(8,128)}, u32[]{:S(2)}) %copy-start.5) | copy-done | bytes 2097176
  141.9 9.5 %adam.1 = (f32[1024,512]{1,0:T(8,128)}, f32[1024,512]{1,0:T(8,128)}, f32[1024,512]{1,0:T(8,128)}) custom-call(s32[1,4096]{1,0:T(1,128)S(1)} %reshape.17.index_ref, s32[4,1,256]{2,1,0:T(1,128)S(1)} %bitcast.16, bf16[4096,512]{1,0:T(8,128)(2,1)} %bitcast.9.arrived_ref, f32[1024,512]{1,0:T(8,128)S(1)} %copy-done.3, f32[1024,512]{1,0:T(8,128)S(1)} %copy-done.4, ...), custom_call_target="tpu_custom_call" | custom-call | tf_op jit(solution)/shard_map/adam/pallas_call | solution.py:218
  151.5 4.0 %place_blocks.1 = bf16[2,4096,256]{2,1,0:T(8,128)(2,1)} custom-call(s32[6]{0:T(128)S(1)} %stack.42.place_ref, bf16[4,256,256]{2,1,0:T(8,128)(2,1)S(1)} %pad_maximum_fusion.refs_0_, bf16[4,256,256]{2,1,0:T(8,128)(2,1)S(1)} %collective-permute-done.13.refs_1_, bf16[4,256,256]{2,1,0:T(8,128)(2,1)} %collective-permute-done.14.refs_2_, ...), custom_call_target="tpu_custom_call" | custom-call | tf_op jit(solution)/shard_map/place_blocks/pallas_call | solution.py:178
  (48 shorter events, 4.1 us)
Async XLA Ops:
  0.8 2.2 %copy-start.1 = (bf16[256,2,4096]{2,1,0:T(2,128)(2,1)S(1)}, bf16[256,2,4096]{2,1,0:T(2,128)(2,1)}, u32[]{:S(2)}) copy-start(bf16[256,2,4096]{2,1,0:T(2,128)(2,1)} %score_ref.1) | copy-start | bytes 12582916
  3.0 0.9 copy-start.6
  3.9 6.2 %copy-start.2 = (bf16[256,4096]{1,0:T(8,128)(2,1)S(1)}, bf16[256,4096]{1,0:T(8,128)(2,1)}, u32[]{:S(2)}) copy-start(bf16[256,4096]{1,0:T(8,128)(2,1)} %grad_ref.1) | copy-start | bytes 6291460
  3.9 6.2 %copy-start.7 = (s32[256,32]{0,1:T(8,128)S(1)}, s32[256,32]{0,1:T(8,128)}, u32[]{:S(2)}) copy-start(s32[256,32]{0,1:T(8,128)} %param.12) | copy-start | bytes 98308
  3.9 6.2 %copy-start.8 = (f32[256,32]{0,1:T(8,128)S(1)}, f32[256,32]{0,1:T(8,128)}, u32[]{:S(2)}) copy-start(f32[256,32]{0,1:T(8,128)} %param.11) | copy-start | bytes 98308
  8.6 8.0 %collective-permute-start = (bf16[4,4,256,256]{3,2,1,0:T(8,128)(2,1)S(1)}, bf16[4,4,256,256]{3,2,1,0:T(8,128)(2,1)S(1)}, u32[]{:S(2)}, u32[]{:S(2)}) collective-permute-start(bf16[4,4,256,256]{3,2,1,0:T(8,128)(2,1)S(1)} %get-tuple-element.27), channel_id=1, source_target_pairs={{0,16},{1,17},{2,18},{3,19},{4,20},{5,21},{6,22},{7,23},{8,24},{9,... | collective-permute-start | bytes 6291464 | tf_op jit(solution)/shard_map/ppermute | solution.py:37
  14.7 2.0 %copy-start = (bf16[128,32,512]{2,1,0:T(8,128)(2,1)}, bf16[128,32,512]{2,1,0:T(8,128)(2,1)S(1)}, u32[]{:S(2)}) copy-start(bf16[128,32,512]{2,1,0:T(8,128)(2,1)S(1)} %combine.1) | copy-start | bytes 12582916
  18.8 119.9 %all-to-all-start = ((bf16[128,32,512]{2,1,0:T(8,128)(2,1)}), bf16[128,32,512]{2,1,0:T(8,128)(2,1)}, u32[]{:S(2)}, u32[]{:S(2)}) async-start(bf16[128,32,512]{2,1,0:T(8,128)(2,1)} %copy-done), calls=%async_computation | async-start | bytes 8388608 | tf_op jit(solution)/shard_map/all_to_all | solution.py:272
  29.4 109.0 %copy-start.12 = (s32[1,128,32]{1,2,0:T(8,128)S(1)}, s32[1,128,32]{1,2,0:T(8,128)}, u32[]{:S(2)}) copy-start(s32[1,128,32]{1,2,0:T(8,128)} %param.13) | copy-start | bytes 49156
  29.4 109.2 %copy-start.3 = (f32[1024,512]{1,0:T(8,128)S(1)}, f32[1024,512]{1,0:T(8,128)}, u32[]{:S(2)}) copy-start(f32[1024,512]{1,0:T(8,128)} %v_ref.1) | copy-start | bytes 6291460
  29.5 109.2 %copy-start.9 = (s32[1024]{0:T(1024)S(1)}, s32[1024]{0:T(1024)}, u32[]{:S(2)}) copy-start(s32[1024]{0:T(1024)} %param.17) | copy-start | bytes 12292
  29.5 54.1 %collective-permute-start.1 = (bf16[4,256,256]{2,1,0:T(8,128)(2,1)}, bf16[4,256,256]{2,1,0:T(8,128)(2,1)S(1)}, u32[]{:S(2)}, u32[]{:S(2)}) collective-permute-start(bf16[4,256,256]{2,1,0:T(8,128)(2,1)} %copy-done.11), channel_id=1, source_target_pairs={{0,32},{1,33},{2,34},{3,35},{4,36},{5,37},{6,38},{7,39},{8,40},{9,... | collective-permute-start | bytes 1572872 | tf_op jit(solution)/shard_map/ppermute | solution.py:37
  31.0 60.0 %collective-permute-start.2 = (bf16[4,256,256]{2,1,0:T(8,128)(2,1)}, bf16[4,256,256]{2,1,0:T(8,128)(2,1)S(1)}, u32[]{:S(2)}, u32[]{:S(2)}) collective-permute-start(bf16[4,256,256]{2,1,0:T(8,128)(2,1)} %copy-done.10), channel_id=1, source_target_pairs={{0,64},{1,65},{2,66},{3,67},{4,68},{5,69},{6,70},{7,71},{8,72},{9,... | collective-permute-start | bytes 1572872 | tf_op jit(solution)/shard_map/ppermute | solution.py:37
  34.0 57.1 %collective-permute-start.3 = (bf16[4,256,256]{2,1,0:T(8,128)(2,1)S(1)}, bf16[4,256,256]{2,1,0:T(8,128)(2,1)S(1)}, u32[]{:S(2)}, u32[]{:S(2)}) collective-permute-start(bf16[4,256,256]{2,1,0:T(8,128)(2,1)S(1)} %get-tuple-element.43), channel_id=1, source_target_pairs={{0,96},{1,97},{2,98},{3,99},{4,100},{5,101},{6,102},{7,103},{8,104... | collective-permute-start | bytes 1572872 | tf_op jit(solution)/shard_map/ppermute | solution.py:37
  91.3 4.4 %collective-permute-start.6 = (bf16[256,256]{1,0:T(8,128)(2,1)S(1)}, bf16[256,256]{1,0:T(8,128)(2,1)S(1)}, u32[]{:S(2)}, u32[]{:S(2)}) collective-permute-start(bf16[256,256]{1,0:T(8,128)(2,1)S(1)} %get-tuple-element.47), channel_id=1, source_target_pairs={{0,12},{1,13},{2,14},{3,15},{4,0},{5,1},{6,2},{7,3},{8,4},{9,5},{1... | collective-permute-start | bytes 393224 | tf_op jit(solution)/shard_map/ppermute | solution.py:37
  93.8 6.4 %collective-permute-start.5 = (bf16[256,256]{1,0:T(8,128)(2,1)S(1)}, bf16[256,256]{1,0:T(8,128)(2,1)S(1)}, u32[]{:S(2)}, u32[]{:S(2)}) collective-permute-start(bf16[256,256]{1,0:T(8,128)(2,1)S(1)} %get-tuple-element.46), channel_id=1, source_target_pairs={{0,4},{1,5},{2,6},{3,7},{4,8},{5,9},{6,10},{7,11},{8,12},{9,13},{1... | collective-permute-start | bytes 393224 | tf_op jit(solution)/shard_map/ppermute | solution.py:37
  93.8 6.4 %collective-permute-start.4 = (bf16[256,256]{1,0:T(8,128)(2,1)S(1)}, bf16[256,256]{1,0:T(8,128)(2,1)S(1)}, u32[]{:S(2)}, u32[]{:S(2)}) collective-permute-start(bf16[256,256]{1,0:T(8,128)(2,1)S(1)} %get-tuple-element.45), channel_id=1, source_target_pairs={{0,8},{1,9},{2,10},{3,11},{4,12},{5,13},{6,14},{7,15},{8,0},{9,1},... | collective-permute-start | bytes 393224 | tf_op jit(solution)/shard_map/ppermute | solution.py:37
  100.3 4.2 %collective-permute-start.9 = (bf16[256,256]{1,0:T(8,128)(2,1)S(1)}, bf16[256,256]{1,0:T(8,128)(2,1)S(1)}, u32[]{:S(2)}, u32[]{:S(2)}) collective-permute-start(bf16[256,256]{1,0:T(8,128)(2,1)S(1)} %add_convert_fusion.1), channel_id=1, source_target_pairs={{0,3},{1,0},{2,1},{3,2},{4,7},{5,4},{6,5},{7,6},{8,11},{9,8},{10,9... | collective-permute-start | bytes 393224 | tf_op jit(solution)/shard_map/ppermute | solution.py:37
  102.0 6.7 %collective-permute-start.8 = (bf16[256,256]{1,0:T(8,128)(2,1)S(1)}, bf16[256,256]{1,0:T(8,128)(2,1)S(1)}, u32[]{:S(2)}, u32[]{:S(2)}) collective-permute-start(bf16[256,256]{1,0:T(8,128)(2,1)S(1)} %add_convert_fusion.1), channel_id=1, source_target_pairs={{0,1},{1,2},{2,3},{3,0},{4,5},{5,6},{6,7},{7,4},{8,9},{9,10},{10,1... | collective-permute-start | bytes 393224 | tf_op jit(solution)/shard_map/ppermute | solution.py:37
  102.0 6.7 %collective-permute-start.7 = (bf16[256,256]{1,0:T(8,128)(2,1)S(1)}, bf16[256,256]{1,0:T(8,128)(2,1)S(1)}, u32[]{:S(2)}, u32[]{:S(2)}) collective-permute-start(bf16[256,256]{1,0:T(8,128)(2,1)S(1)} %add_convert_fusion.1), channel_id=1, source_target_pairs={{0,2},{1,3},{2,0},{3,1},{4,6},{5,7},{6,4},{7,5},{8,10},{9,11},{10,... | collective-permute-start | bytes 393224 | tf_op jit(solution)/shard_map/ppermute | solution.py:37
  108.8 6.8 %collective-permute-start.12 = (bf16[256,256]{1,0:T(8,128)(2,1)S(1)}, bf16[256,256]{1,0:T(8,128)(2,1)S(1)}, u32[]{:S(2)}, u32[]{:S(2)}) collective-permute-start(bf16[256,256]{1,0:T(8,128)(2,1)S(1)} %add_convert_fusion), channel_id=1, source_target_pairs={{0,32},{1,33},{2,34},{3,35},{4,36},{5,37},{6,38},{7,39},{8,40},{9,... | collective-permute-start | bytes 393224 | tf_op jit(solution)/shard_map/ppermute | solution.py:37
  108.8 6.7 %collective-permute-start.11 = (bf16[256,256]{1,0:T(8,128)(2,1)S(1)}, bf16[256,256]{1,0:T(8,128)(2,1)S(1)}, u32[]{:S(2)}, u32[]{:S(2)}) collective-permute-start(bf16[256,256]{1,0:T(8,128)(2,1)S(1)} %add_convert_fusion), channel_id=1, source_target_pairs={{0,64},{1,65},{2,66},{3,67},{4,68},{5,69},{6,70},{7,71},{8,72},{9,... | collective-permute-start | bytes 393224 | tf_op jit(solution)/shard_map/ppermute | solution.py:37
  110.3 5.8 %collective-permute-start.10 = (bf16[256,256]{1,0:T(8,128)(2,1)S(1)}, bf16[256,256]{1,0:T(8,128)(2,1)S(1)}, u32[]{:S(2)}, u32[]{:S(2)}) collective-permute-start(bf16[256,256]{1,0:T(8,128)(2,1)S(1)} %add_convert_fusion), channel_id=1, source_target_pairs={{0,96},{1,97},{2,98},{3,99},{4,100},{5,101},{6,102},{7,103},{8,104... | collective-permute-start | bytes 393224 | tf_op jit(solution)/shard_map/ppermute | solution.py:37
  116.2 8.6 %collective-permute-start.13 = (bf16[4,256,256]{2,1,0:T(8,128)(2,1)S(1)}, bf16[4,256,256]{2,1,0:T(8,128)(2,1)S(1)}, u32[]{:S(2)}, u32[]{:S(2)}) collective-permute-start(bf16[4,256,256]{2,1,0:T(8,128)(2,1)S(1)} %pad_maximum_fusion.refs_0_), channel_id=1, source_target_pairs={{0,12},{1,13},{2,14},{3,15},{4,0},{5,1},{6,2},{7,3},{8,4},{9,5},{1... | collective-permute-start | bytes 1572872 | tf_op jit(solution)/shard_map/ppermute | solution.py:37
  117.5 12.4 %collective-permute-start.14 = (bf16[4,256,256]{2,1,0:T(8,128)(2,1)S(1)}, bf16[4,256,256]{2,1,0:T(8,128)(2,1)}, u32[]{:S(2)}, u32[]{:S(2)}) collective-permute-start(bf16[4,256,256]{2,1,0:T(8,128)(2,1)S(1)} %pad_maximum_fusion.refs_0_), channel_id=1, source_target_pairs={{0,8},{1,9},{2,10},{3,11},{4,12},{5,13},{6,14},{7,15},{8,0},{9,1},... | collective-permute-start | bytes 1572872 | tf_op jit(solution)/shard_map/ppermute | solution.py:37
  117.6 15.4 %collective-permute-start.15 = (bf16[4,256,256]{2,1,0:T(8,128)(2,1)S(1)}, bf16[4,256,256]{2,1,0:T(8,128)(2,1)}, u32[]{:S(2)}, u32[]{:S(2)}) collective-permute-start(bf16[4,256,256]{2,1,0:T(8,128)(2,1)S(1)} %pad_maximum_fusion.refs_0_), channel_id=1, source_target_pairs={{0,4},{1,5},{2,6},{3,7},{4,8},{5,9},{6,10},{7,11},{8,12},{9,13},{1... | collective-permute-start | bytes 1572872 | tf_op jit(solution)/shard_map/ppermute | solution.py:37
  118.2 33.2 %collective-permute-start.16 = (bf16[4,256,256]{2,1,0:T(8,128)(2,1)S(1)}, bf16[4,256,256]{2,1,0:T(8,128)(2,1)}, u32[]{:S(2)}, u32[]{:S(2)}) collective-permute-start(bf16[4,256,256]{2,1,0:T(8,128)(2,1)S(1)} %pad_maximum_fusion.refs_0_), channel_id=1, source_target_pairs={{0,16},{1,17},{2,18},{3,19},{4,20},{5,21},{6,22},{7,23},{8,24},{9,... | collective-permute-start | bytes 1572872 | tf_op jit(solution)/shard_map/ppermute | solution.py:37
  124.9 26.6 %collective-permute-start.17 = (bf16[4,256,256]{2,1,0:T(8,128)(2,1)S(1)}, bf16[4,256,256]{2,1,0:T(8,128)(2,1)}, u32[]{:S(2)}, u32[]{:S(2)}) collective-permute-start(bf16[4,256,256]{2,1,0:T(8,128)(2,1)S(1)} %collective-permute-done.13.refs_1_), channel_id=1, source_target_pairs={{0,16},{1,17},{2,18},{3,19},{4,20},{5,21},{6,22},{7,23},{8,24},{9,... | collective-permute-start | bytes 1572872 | tf_op jit(solution)/shard_map/ppermute | solution.py:37
  129.9 21.5 %collective-permute-start.18 = (bf16[4,256,256]{2,1,0:T(8,128)(2,1)}, bf16[4,256,256]{2,1,0:T(8,128)(2,1)}, u32[]{:S(2)}, u32[]{:S(2)}) collective-permute-start(bf16[4,256,256]{2,1,0:T(8,128)(2,1)} %collective-permute-done.14.refs_2_), channel_id=1, source_target_pairs={{0,16},{1,17},{2,18},{3,19},{4,20},{5,21},{6,22},{7,23},{8,24},{9,... | collective-permute-start | bytes 1572872 | tf_op jit(solution)/shard_map/ppermute | solution.py:37
  132.9 18.5 %collective-permute-start.19 = (bf16[4,256,256]{2,1,0:T(8,128)(2,1)}, bf16[4,256,256]{2,1,0:T(8,128)(2,1)}, u32[]{:S(2)}, u32[]{:S(2)}) collective-permute-start(bf16[4,256,256]{2,1,0:T(8,128)(2,1)} %collective-permute-done.15.refs_3_), channel_id=1, source_target_pairs={{0,16},{1,17},{2,18},{3,19},{4,20},{5,21},{6,22},{7,23},{8,24},{9,... | collective-permute-start | bytes 1572872 | tf_op jit(solution)/shard_map/ppermute | solution.py:37
  138.7 1.6 %copy-start.4 = (f32[1024,512]{1,0:T(8,128)S(1)}, f32[1024,512]{1,0:T(8,128)}, u32[]{:S(2)}) copy-start(f32[1024,512]{1,0:T(8,128)} %m_ref.1) | copy-start | bytes 6291460
  140.3 1.6 %copy-start.5 = (f32[1024,512]{1,0:T(8,128)S(1)}, f32[1024,512]{1,0:T(8,128)}, u32[]{:S(2)}) copy-start(f32[1024,512]{1,0:T(8,128)} %s_ref.1) | copy-start | bytes 6291460
  (2 other events, 1.6 us)

commit v2 on v1

--- a/solution.py
+++ b/solution.py
@@ -37,7 +37,14 @@
     return lax.ppermute(value, AXES, pairs)
 
 
-def combine_kernel(pos_ref, weight_ref, grad_ref, out_ref, mix_ref):
+def in_hbm(value):
+    return pltpu.with_memory_space_constraint(value, pltpu.HBM)
+
+
+BESIDE_TRANSFER = pl.CostEstimate(flops=10**11, bytes_accessed=0, transcendentals=0)
+
+
+def first_kernel(pos_ref, weight_ref, grad_ref, out_ref, mix_ref):
     slots, tokens = pos_ref.shape
     rows = mix_ref.shape[0]
     step = 64
@@ -60,24 +67,46 @@
     out_ref[...] = product.astype(BF).reshape(out_ref.shape)
 
 
-def combine(slot_pos, slot_weight, grad_out, n_data, n_table, cap):
+def next_kernel(mix_ref, grad_ref, out_ref):
+    product = jnp.dot(mix_ref[...], grad_ref[...], preferred_element_type=F32)
+    out_ref[...] = product.astype(BF).reshape(out_ref.shape)
+
+
+def combine(slot_pos, slot_weight, grad_out, n_data, n_table, cap, pieces):
     tokens, width = grad_out.shape
-    slots = slot_pos.shape[1]
-    columns = width // n_data
-    return pl.pallas_call(
-        combine_kernel,
+    rows = n_table * cap
+    columns = width // n_data // pieces
+    slots = pl.BlockSpec((slot_pos.shape[1], tokens), lambda i: (0, 0))
+    mixed = pl.BlockSpec((rows, tokens), lambda i: (0, 0))
+    out_spec = pl.BlockSpec((n_table, cap, columns), lambda i: (i, 0, 0))
+    out_shape = pltpu.HBM((n_data * n_table, cap, columns), BF)
+    params = pltpu.CompilerParams(vmem_limit_bytes=32 << 20)
+
+    def grad(k):
+        return pl.BlockSpec((tokens, columns), lambda i: (0, i * pieces + k))
+
+    first, mix = pl.pallas_call(
+        first_kernel,
         grid=(n_data,),
-        in_specs=[
-            pl.BlockSpec((slots, tokens), lambda i: (0, 0)),
-            pl.BlockSpec((slots, tokens), lambda i: (0, 0)),
-            pl.BlockSpec((tokens, columns), lambda i: (0, i)),
-        ],
-        out_specs=pl.BlockSpec((n_table, cap, columns), lambda i: (i, 0, 0)),
-        out_shape=jax.ShapeDtypeStruct((n_data * n_table, cap, columns), BF),
-        scratch_shapes=[pltpu.VMEM((n_table * cap, tokens), BF)],
-        compiler_params=pltpu.CompilerParams(vmem_limit_bytes=32 << 20),
-        name="combine",
+        in_specs=[slots, slots, grad(0)],
+        out_specs=[out_spec, mixed],
+        out_shape=[out_shape, pltpu.HBM((rows, tokens), BF)],
+        compiler_params=params,
+        name="combine_first",
     )(slot_pos.T, slot_weight.T, grad_out)
+    rest = [
+        pl.pallas_call(
+            next_kernel,
+            grid=(n_data,),
+            in_specs=[mixed, grad(k)],
+            out_specs=out_spec,
+            out_shape=out_shape,
+            compiler_params=params,
+            name="combine_next",
+        )(mix, grad_out)
+        for k in range(1, pieces)
+    ]
+    return [first, *rest]
 
 
 def partials_kernel(place_ref, score_ref, query_ref, own_ref, other_ref):
@@ -116,7 +145,7 @@
         out_shape=[shape] * 2,
         compiler_params=pltpu.CompilerParams(vmem_limit_bytes=32 << 20),
         name="partials",
-    )(places, score, query)
+    )(places, score, in_hbm(query))
 
 
 def merge_kernel(own_ref, got_ref, *out_refs):
@@ -140,33 +169,49 @@
         out_ref[...] = (near + far).astype(BF)
 
 
-def sum_chunks(chunks):
-    shape = jax.ShapeDtypeStruct(chunks[0].shape[1:], BF)
+def sum_chunks(chunks, cost=None):
+    shape = pltpu.HBM(chunks[0].shape[1:], BF)
     return pl.pallas_call(
         sum_kernel,
         out_shape=[shape] * 4,
+        cost_estimate=cost,
         compiler_params=pltpu.CompilerParams(vmem_limit_bytes=32 << 20),
         name="sum_chunks",
     )(*chunks)
 
 
+def sum_all_kernel(a_ref, b_ref, c_ref, d_ref, out_ref):
+    near = a_ref[...].astype(F32) + c_ref[...].astype(F32)
+    far = b_ref[...].astype(F32) + d_ref[...].astype(F32)
+    out_ref[...] = (near + far).astype(BF)
+
+
+def sum_all(chunks, cost=None):
+    return pl.pallas_call(
+        sum_all_kernel,
+        out_shape=jax.ShapeDtypeStruct(chunks[0].shape, BF),
+        cost_estimate=cost,
+        name="sum_all",
+    )(*chunks)
+
+
 def place_kernel(place_ref, *refs):
-    blocks, (out_ref, held, sem_in, sem_out) = refs[:8], refs[8:]
-    loads = [pltpu.make_async_copy(blocks[k], held.at[k], sem_in.at[k]) for k in range(8)]
+    blocks = refs[:4]
+    out_ref, held, sem_in, sem_out = refs[-4:]
+    loads = [pltpu.make_async_copy(blocks[k], held.at[k], sem_in.at[k]) for k in range(4)]
     for load in loads:
         load.start()
     stores = []
-    for k in range(8):
-        half, rb = k // 4, k % 4
-        loads[k].wait()
+    for rb in range(4):
+        loads[rb].wait()
         for ra in range(4):
-            a = (place_ref[3 * half + 1] + ra) % 4
-            b = (place_ref[3 * half + 2] + rb) % 4
+            a = (place_ref[1] + ra) % 4
+            b = (place_ref[2] + rb) % 4
             start = pl.multiple_of((a * 4 + b) * 256, 256)
             store = pltpu.make_async_copy(
-                held.at[k, ra],
-                out_ref.at[place_ref[3 * half], pl.ds(start, 256)],
-                sem_out.at[k * 4 + ra],
+                held.at[rb, ra],
+                out_ref.at[place_ref[0], pl.ds(start, 256)],
+                sem_out.at[rb * 4 + ra],
             )
             store.start()
             stores.append(store)
@@ -174,29 +219,35 @@
         store.wait()
 
 
-def place_blocks(places, buffers):
+def place_half(place, buffers, out=()):
     return pl.pallas_call(
         place_kernel,
-        in_specs=[pl.BlockSpec(memory_space=pltpu.SMEM)] + [pl.BlockSpec(memory_space=pl.ANY)] * 8,
+        in_specs=[pl.BlockSpec(memory_space=pltpu.SMEM)]
+        + [pl.BlockSpec(memory_space=pl.ANY)] * (4 + len(out)),
         out_specs=pl.BlockSpec(memory_space=pl.ANY),
         out_shape=jax.ShapeDtypeStruct((2, 4096, 256), BF),
+        input_output_aliases={5: 0} if out else {},
         scratch_shapes=[
-            pltpu.VMEM((8, *buffers[0].shape), BF),
-            pltpu.SemaphoreType.DMA((8,)),
-            pltpu.SemaphoreType.DMA((32,)),
+            pltpu.VMEM((4, *buffers[0].shape), BF),
+            pltpu.SemaphoreType.DMA((4,)),
+            pltpu.SemaphoreType.DMA((16,)),
         ],
         compiler_params=pltpu.CompilerParams(vmem_limit_bytes=16 << 20),
-        name="place_blocks",
-    )(places, *buffers)
-
-
-def adam_kernel(index_ref, steps_ref, arrived_ref, v_ref, m_ref, s_ref, nv_ref, nm_ref, ns_ref):
-    rows, columns = v_ref.shape
+        name="place_half",
+    )(place, *buffers, *out)
+
+
+def adam_kernel(index_ref, steps_ref, *refs):
+    rows = steps_ref.shape[2]
     slots = index_ref.shape[1]
+    v_ref, m_ref, s_ref = refs[-6:-3] if len(refs) < 9 else refs[-9:-6]
+    nv_ref, nm_ref, ns_ref = refs[-3:]
+    arrived = refs[: len(refs) - (6 if len(refs) < 9 else 9)]
     base = pl.program_id(0) * rows
     place = lax.broadcasted_iota(jnp.int32, (rows, slots), 0) + base
     selector = jnp.where(index_ref[...] == place, 1.0, 0.0).astype(BF)
-    grad = jnp.dot(selector, arrived_ref[...], preferred_element_type=F32)
+    grad = [jnp.dot(selector, a[...], preferred_element_type=F32) for a in arrived]
+    grad = grad[0] if len(grad) == 1 else jnp.concatenate(grad, axis=1)
     steps = steps_ref[0].astype(F32)
     first = 1.0 / (1.0 - jnp.exp(steps * jnp.log(jnp.float32(0.9))))
     second = 1.0 / (1.0 - jnp.exp(steps * jnp.log(jnp.float32(0.95))))
@@ -209,28 +260,45 @@
     nv_ref[...] = v_ref[...] - 0.1 * (new_first * first) / (jnp.sqrt(new_second * second) + 1e-08)
 
 
-def adam(index, steps, arrived, values, first_moment, second_moment):
-    owned, columns = values.shape
-    rows = 256
+def adam(index, steps, arrived, state, column, done=(), cost=None):
+    owned = state[0].shape[0]
+    rows = steps.shape[2]
     slots = index.shape[1]
-    block = pl.BlockSpec((rows, columns), lambda i: (i, 0))
-    shape = jax.ShapeDtypeStruct(values.shape, F32)
+    width = sum(a.shape[1] for a in arrived)
+    block = pl.BlockSpec((rows, width), lambda i: (i, column))
+    shape = jax.ShapeDtypeStruct(state[0].shape, F32)
+    before = 2 + len(arrived) + 3
     return pl.pallas_call(
         adam_kernel,
         grid=(owned // rows,),
         in_specs=[
             pl.BlockSpec((1, slots), lambda i: (0, 0)),
             pl.BlockSpec((1, 1, rows), lambda i: (i, 0, 0)),
-            pl.BlockSpec((slots, columns), lambda i: (0, 0)),
-            block,
-            block,
-            block,
-        ],
+        ]
+        + [pl.BlockSpec(a.shape, lambda i: (0, 0)) for a in arrived]
+        + [block] * 3
+        + [pl.BlockSpec(memory_space=pl.ANY)] * len(done),
         out_specs=[block] * 3,
         out_shape=[shape] * 3,
+        input_output_aliases={before + k: k for k in range(len(done))},
+        cost_estimate=cost,
         compiler_params=pltpu.CompilerParams(vmem_limit_bytes=40 << 20),
         name="adam",
-    )(index, steps, arrived, values, first_moment, second_moment)
+    )(index, steps, *arrived, *[in_hbm(x) for x in state], *done)
+
+
+def stack_kernel(*refs):
+    for k, ref in enumerate(refs[:-1]):
+        refs[-1][k] = ref[...]
+
+
+def stack(blocks, cost=None):
+    return pl.pallas_call(
+        stack_kernel,
+        out_shape=pltpu.HBM((len(blocks), *blocks[0].shape), BF),
+        cost_estimate=cost,
+        name="stack",
+    )(*blocks)
 
 
 def places_of():
@@ -260,36 +328,40 @@
     n_table = lax.axis_size("table")
     n_data = lax.axis_size("dp")
     cap = slot_rows.shape[2]
-    columns = values.shape[1]
     places = places_of()
+
+    def exchange(ordered):
+        moved = lax.all_to_all(ordered, AXES, split_axis=0, concat_axis=0, tiled=True)
+        return moved.reshape(-1, moved.shape[2])
 
     own, other = partials(places, score_grad, queries)
     got = send(other, SWAP)
-    ordered = combine(slot_pos, slot_weight, grad_out, n_data, n_table, cap)
+    ordered = combine(slot_pos, slot_weight, grad_out, n_data, n_table, cap, 2)
     chunks = merge(own, got)
-    ordered, chunks = lax.optimization_barrier((ordered, chunks))
+    ordered[0], chunks = lax.optimization_barrier((ordered[0], chunks))
     chunks = [chunks[0]] + [send(chunks[r], ring(0, r)) for r in (1, 2, 3)]
-    arrived = lax.all_to_all(ordered, AXES, split_axis=0, concat_axis=0, tiled=True)
-    parts = sum_chunks(chunks)
+    arrived = [exchange(ordered[0])]
+    parts = sum_chunks(chunks, BESIDE_TRANSFER)
     parts = [parts[0]] + [send(parts[r], ring(1, r)) for r in (1, 2, 3)]
-    near = parts[0].astype(F32) + parts[2].astype(F32)
-    total = (near + (parts[1].astype(F32) + parts[3].astype(F32))).astype(BF)
-    around = [send(total, ring(2, r)) for r in (1, 2, 3)]
-    near = total.astype(F32) + around[1].astype(F32)
-    final = (near + (around[0].astype(F32) + around[2].astype(F32))).astype(BF)
-    mine = jnp.stack([final] + [send(final, ring(0, -r)) for r in (1, 2, 3)])
+    total = sum_all(parts)
+    ordered[1], total = lax.optimization_barrier((ordered[1], total))
+    around = [total] + [send(total, ring(2, r)) for r in (1, 2, 3)]
+    arrived.append(exchange(ordered[1]))
+    final = sum_all(around, BESIDE_TRANSFER)
+    mine = [final] + [send(final, ring(0, -r)) for r in (1, 2, 3)]
+
+    index = slot_rows.reshape(1, -1)
+    steps = row_steps.reshape(-1, 1, 256)
+    state = (values, first_moment, second_moment)
+    outs = adam(index, steps, arrived[:1], state, 0)
+    mine, outs = lax.optimization_barrier((mine, outs))
+    mine = jnp.stack(mine)
     buffers = [mine] + [send(mine, ring(1, -r)) for r in (1, 2, 3)]
-    buffers += [send(b, SWAP) for b in buffers]
-    outs = adam(
-        slot_rows.reshape(1, -1),
-        row_steps.reshape(-1, 1, 256),
-        arrived.reshape(-1, columns),
-        values,
-        first_moment,
-        second_moment,
-    )
-    places, outs = lax.optimization_barrier((places, outs))
-    subkey_out = place_blocks(places, buffers)
+    outs = adam(index, steps, arrived[1:], state, 1, outs)
+    buffers[1:], outs = lax.optimization_barrier((buffers[1:], outs))
+    theirs = [send(b, SWAP) for b in buffers]
+    subkey_out = place_half(places[:3], buffers)
+    subkey_out = place_half(places[3:], theirs, (subkey_out,))
     return (*outs, subkey_out)
 
 

time: 156 us -> 135 us (0.87)
  waiting for transfers between devices: 70.4 us -> 32.7 us
  Pallas kernels: 23.5 us -> 41.7 us
  local copies, waits for them, and re-layouts: 10.2 us -> 4.52 us
  starting transfers between devices: 50.3 us -> 54.5 us
    ppermute x20, waiting for transfers between devices: 70.4 us -> 32.6 us  [send(): return lax.ppermute(value, AXES, pairs)]
    pallas_call x3 -> x7, Pallas kernels: 8.78 us -> 22 us  [the longest x2 6.21 us: place_half(): pl.pallas_call(place_kernel, in_specs=[pl.BlockSpec(memory_space=pltpu.SM...]
    unnamed x27 -> x29, local copies, waits for them, and re-layouts: 10 us -> 4.34 us
    pallas_call x1 -> x2, Pallas kernels: 9.55 us -> 12.8 us  [adam(): pl.pallas_call(adam_kernel, grid=(owned // rows,), in_specs=[pl.BlockSpec...]
    all_to_all x1 -> x2, starting transfers between devices: 10.7 us -> 12.8 us  [exchange(): lax.all_to_all(ordered, AXES, split_axis=0, concat_axis=0, tiled=True)]
    ppermute x20, starting transfers between devices: 39.6 us -> 41.7 us  [send(): return lax.ppermute(value, AXES, pairs)]
  transfers between devices with their start and end apart: 21 -> 22, of which waited for: 8 -> 8; matrix products, arithmetic and copies ran while one was open for 0% -> 0% of each run, Pallas kernels for 9% -> 24%
where the time goes in v2:
time: 135 us; the launch traced here: 134 us
  starting transfers between devices  54.5 us (40%)
  Pallas kernels  41.7 us (31%)
  waiting for transfers between devices  32.7 us (24%)
  local copies, waits for them, and re-layouts  4.52 us (3%)
    ppermute x20, starting transfers between devices, send(): return lax.ppermute(value, AXES, pairs)  41.7 us
    ppermute x20, waiting for transfers between devices, send(): return lax.ppermute(value, AXES, pairs)  32.6 us
    pallas_call x2, Pallas kernels, adam(): pl.pallas_call(adam_kernel, grid=(owned // rows,), in_specs=[pl.BlockSpec...  12.8 us
    all_to_all x2, starting transfers between devices, exchange(): lax.all_to_all(ordered, AXES, split_axis=0, concat_axis=0, tiled=True)  12.8 us
    pallas_call x2, Pallas kernels, place_half(): pl.pallas_call(place_kernel, in_specs=[pl.BlockSpec(memory_space=pltpu.SM...  6.21 us
    pallas_call x1, Pallas kernels, combine(): pl.pallas_call(first_kernel, grid=(n_data,), in_specs=[slots, slots, grad...  5.97 us
    pallas_call x1, Pallas kernels, partials(): pl.pallas_call(partials_kernel, grid_spec=pltpu.PrefetchScalarGridSpec(nu...  5.51 us
    unnamed x29, local copies, waits for them, and re-layouts  4.34 us
  transfers between devices with their start and end apart: 22, of which 8 were waited for; matrix products, arithmetic and copies ran while one was open for 0% of the time, Pallas kernels for 24%

profile of v2, /device:TPU:1, one launch (start us, length us, event | category | flops | bytes accessed | tf_op | source)
XLA Modules:
  0.0 134.5 jit_solution(17431730068951195196)
XLA Ops:
  0.8 2.2 %copy-done.1 = bf16[256,2,4096]{2,1,0:T(2,128)(2,1)S(1)} copy-done((bf16[256,2,4096]{2,1,0:T(2,128)(2,1)S(1)}, bf16[256,2,4096]{2,1,0:T(2,128)(2,1)}, u32[]{:S(2)}) %copy-start.1) | copy-done | bytes 4194328
  3.0 5.5 %partials.1 = (bf16[4,4,256,256]{3,2,1,0:T(8,128)(2,1)S(1)}, bf16[4,4,256,256]{3,2,1,0:T(8,128)(2,1)S(1)}) custom-call(s32[6]{0:T(128)S(1)} %stack.46.place_ref, bf16[256,2,4096]{2,1,0:T(2,128)(2,1)S(1)} %copy-done.1, bf16[256,2,256]{2,1,0:T(2,128)(2,1)} %query_ref.1), custom_call_target="tpu_custom_call" | custom-call | tf_op jit(solution)/shard_map/partials/pallas_call | solution.py:131
  8.5 1.5 %collective-permute-start = (bf16[4,4,256,256]{3,2,1,0:T(8,128)(2,1)S(1)}, bf16[4,4,256,256]{3,2,1,0:T(8,128)(2,1)S(1)}, u32[]{:S(2)}, u32[]{:S(2)}) collective-permute-start(bf16[4,4,256,256]{3,2,1,0:T(8,128)(2,1)S(1)} %get-tuple-element.45), channel_id=1, source_target_pairs={{0,16},{1,17},{2,18},{3,19},{4,20},{5,21},{6,22},{7,23},{8,24},{9,... | collective-permute-start | bytes 6291464 | tf_op jit(solution)/shard_map/ppermute | solution.py:37
  10.0 6.0 %combine_first.1 = (bf16[128,32,256]{2,1,0:T(8,128)(2,1)}, bf16[512,256]{1,0:T(8,128)(2,1)}) custom-call(s32[32,256]{1,0:T(8,128)S(1)} %bitcast.16, f32[32,256]{1,0:T(8,128)S(1)} %bitcast.17, bf16[256,4096]{1,0:T(8,128)(2,1)S(1)} %copy-done), custom_call_target="tpu_custom_call" | custom-call | tf_op jit(solution)/shard_map/combine_first/pallas_call | solution.py:88
  16.0 1.4 %merge.1 = (bf16[4,256,256]{2,1,0:T(8,128)(2,1)S(1)}, bf16[4,256,256]{2,1,0:T(8,128)(2,1)}, bf16[4,256,256]{2,1,0:T(8,128)(2,1)}, bf16[4,256,256]{2,1,0:T(8,128)(2,1)}) custom-call(bf16[4,4,256,256]{3,2,1,0:T(8,128)(2,1)S(1)} %get-tuple-element.44.own_ref, bf16[4,4,256,256]{3,2,1,0:T(8,128)(2,1)S(1)} %collective-permute-done.got_ref), custom_call_target="tpu_custom_call" | custom-call | tf_op jit(solution)/shard_map/merge/pallas_call | solution.py:157
  17.4 1.7 %collective-permute-start.1 = (bf16[4,256,256]{2,1,0:T(8,128)(2,1)}, bf16[4,256,256]{2,1,0:T(8,128)(2,1)S(1)}, u32[]{:S(2)}, u32[]{:S(2)}) collective-permute-start(bf16[4,256,256]{2,1,0:T(8,128)(2,1)} %get-tuple-element.51), channel_id=1, source_target_pairs={{0,32},{1,33},{2,34},{3,35},{4,36},{5,37},{6,38},{7,39},{8,40},{9,... | collective-permute-start | bytes 1572872 | tf_op jit(solution)/shard_map/ppermute | solution.py:37
  19.1 3.3 %collective-permute-start.2 = (bf16[4,256,256]{2,1,0:T(8,128)(2,1)}, bf16[4,256,256]{2,1,0:T(8,128)(2,1)}, u32[]{:S(2)}, u32[]{:S(2)}) collective-permute-start(bf16[4,256,256]{2,1,0:T(8,128)(2,1)} %get-tuple-element.52), channel_id=1, source_target_pairs={{0,64},{1,65},{2,66},{3,67},{4,68},{5,69},{6,70},{7,71},{8,72},{9,... | collective-permute-start | bytes 1572872 | tf_op jit(solution)/shard_map/ppermute | solution.py:37
  23.1 8.0 %all-to-all-start = ((bf16[128,32,256]{2,1,0:T(8,128)(2,1)}), bf16[128,32,256]{2,1,0:T(8,128)(2,1)}, u32[]{:S(2)}, u32[]{:S(2)}) async-start(bf16[128,32,256]{2,1,0:T(8,128)(2,1)} %get-tuple-element.59), calls=%async_computation | async-start | bytes 4194304 | tf_op jit(solution)/shard_map/all_to_all | solution.py:334
  31.2 4.0 %collective-permute-done.2.c_ref = bf16[4,256,256]{2,1,0:T(8,128)(2,1)} collective-permute-done((bf16[4,256,256]{2,1,0:T(8,128)(2,1)}, bf16[4,256,256]{2,1,0:T(8,128)(2,1)}, u32[]{:S(2)}, u32[]{:S(2)}) %collective-permute-start.2) | collective-permute-done | bytes 524320 | tf_op jit(solution)/shard_map/ppermute | solution.py:37
  35.6 2.1 %sum_chunks.1 = (bf16[256,256]{1,0:T(8,128)(2,1)}, bf16[256,256]{1,0:T(8,128)(2,1)}, bf16[256,256]{1,0:T(8,128)(2,1)}, bf16[256,256]{1,0:T(8,128)(2,1)}) custom-call(bf16[4,256,256]{2,1,0:T(8,128)(2,1)S(1)} %get-tuple-element.50.a_ref, bf16[4,256,256]{2,1,0:T(8,128)(2,1)S(1)} %collective-permute-done.1.b_ref, ...), custom_call_target="tpu_custom_call" | custom-call | flops 99999997952 | tf_op jit(solution)/shard_map/sum_chunks/pallas_call | solution.py:174
  37.7 7.4 %collective-permute-start.4 = (bf16[256,256]{1,0:T(8,128)(2,1)}, bf16[256,256]{1,0:T(8,128)(2,1)S(1)}, u32[]{:S(2)}, u32[]{:S(2)}) collective-permute-start(bf16[256,256]{1,0:T(8,128)(2,1)} %get-tuple-element.55), channel_id=1, source_target_pairs={{0,4},{1,5},{2,6},{3,7},{4,8},{5,9},{6,10},{7,11},{8,12},{9,13},{1... | collective-permute-start | bytes 393224 | tf_op jit(solution)/shard_map/ppermute | solution.py:37
  45.0 4.5 %collective-permute-start.5 = (bf16[256,256]{1,0:T(8,128)(2,1)}, bf16[256,256]{1,0:T(8,128)(2,1)S(1)}, u32[]{:S(2)}, u32[]{:S(2)}) collective-permute-start(bf16[256,256]{1,0:T(8,128)(2,1)} %get-tuple-element.56), channel_id=1, source_target_pairs={{0,8},{1,9},{2,10},{3,11},{4,12},{5,13},{6,14},{7,15},{8,0},{9,1},... | collective-permute-start | bytes 393224 | tf_op jit(solution)/shard_map/ppermute | solution.py:37
  49.5 4.1 %combine_next.1 = bf16[128,32,256]{2,1,0:T(8,128)(2,1)} custom-call(bf16[512,256]{1,0:T(8,128)(2,1)S(1)} %copy-done.2, bf16[256,4096]{1,0:T(8,128)(2,1)S(1)} %copy-done), custom_call_target="tpu_custom_call" | custom-call | tf_op jit(solution)/shard_map/combine_next/pallas_call | solution.py:98
  53.6 4.7 %collective-permute-done.4.b_ref = bf16[256,256]{1,0:T(8,128)(2,1)S(1)} collective-permute-done((bf16[256,256]{1,0:T(8,128)(2,1)}, bf16[256,256]{1,0:T(8,128)(2,1)S(1)}, u32[]{:S(2)}, u32[]{:S(2)}) %collective-permute-start.4) | collective-permute-done | bytes 131104 | tf_op jit(solution)/shard_map/ppermute | solution.py:37
  58.3 1.4 %collective-permute-done.5.c_ref = bf16[256,256]{1,0:T(8,128)(2,1)S(1)} collective-permute-done((bf16[256,256]{1,0:T(8,128)(2,1)}, bf16[256,256]{1,0:T(8,128)(2,1)S(1)}, u32[]{:S(2)}, u32[]{:S(2)}) %collective-permute-start.5) | collective-permute-done | bytes 131104 | tf_op jit(solution)/shard_map/ppermute | solution.py:37
  60.4 1.8 %sum_all.2.a_ref = bf16[256,256]{1,0:T(8,128)(2,1)} custom-call(bf16[256,256]{1,0:T(8,128)(2,1)} %get-tuple-element.54.a_ref, bf16[256,256]{1,0:T(8,128)(2,1)} %copy-done.6, bf16[256,256]{1,0:T(8,128)(2,1)} %copy-done.7, bf16[256,256]{1,0:T(8,128)(2,1)} %copy-done.8), custom_call_target="tpu_custom_call" | custom-call | tf_op jit(solution)/shard_map/sum_all/pallas_call | solution.py:190
  62.2 4.1 %collective-permute-start.7 = (bf16[256,256]{1,0:T(8,128)(2,1)}, bf16[256,256]{1,0:T(8,128)(2,1)S(1)}, u32[]{:S(2)}, u32[]{:S(2)}) collective-permute-start(bf16[256,256]{1,0:T(8,128)(2,1)} %sum_all.2.a_ref), channel_id=1, source_target_pairs={{0,1},{1,2},{2,3},{3,0},{4,5},{5,6},{6,7},{7,4},{8,9},{9,10},{10,1... | collective-permute-start | bytes 393224 | tf_op jit(solution)/shard_map/ppermute | solution.py:37
  66.3 6.8 %collective-permute-start.8 = (bf16[256,256]{1,0:T(8,128)(2,1)}, bf16[256,256]{1,0:T(8,128)(2,1)S(1)}, u32[]{:S(2)}, u32[]{:S(2)}) collective-permute-start(bf16[256,256]{1,0:T(8,128)(2,1)} %sum_all.2.a_ref), channel_id=1, source_target_pairs={{0,2},{1,3},{2,0},{3,1},{4,6},{5,7},{6,4},{7,5},{8,10},{9,11},{10,... | collective-permute-start | bytes 393224 | tf_op jit(solution)/shard_map/ppermute | solution.py:37
  73.1 1.6 %collective-permute-start.9 = (bf16[256,256]{1,0:T(8,128)(2,1)}, bf16[256,256]{1,0:T(8,128)(2,1)S(1)}, u32[]{:S(2)}, u32[]{:S(2)}) collective-permute-start(bf16[256,256]{1,0:T(8,128)(2,1)} %sum_all.2.a_ref), channel_id=1, source_target_pairs={{0,3},{1,0},{2,1},{3,2},{4,7},{5,4},{6,5},{7,6},{8,11},{9,8},{10,9... | collective-permute-start | bytes 393224 | tf_op jit(solution)/shard_map/ppermute | solution.py:37
  74.6 4.8 %all-to-all-start.1 = ((bf16[128,32,256]{2,1,0:T(8,128)(2,1)}), bf16[128,32,256]{2,1,0:T(8,128)(2,1)S(1)}, u32[]{:S(2)}, u32[]{:S(2)}) async-start(bf16[128,32,256]{2,1,0:T(8,128)(2,1)} %combine_next.1), calls=%async_computation.1 | async-start | bytes 4194304 | tf_op jit(solution)/shard_map/all_to_all | solution.py:334
  80.8 1.8 %sum_all.3 = bf16[256,256]{1,0:T(8,128)(2,1)} custom-call(bf16[256,256]{1,0:T(8,128)(2,1)} %sum_all.2.a_ref, bf16[256,256]{1,0:T(8,128)(2,1)} %copy-done.11, bf16[256,256]{1,0:T(8,128)(2,1)} %copy-done.12, bf16[256,256]{1,0:T(8,128)(2,1)} %copy-done.13), custom_call_target="tpu_custom_call" | custom-call | flops 99999997952 | tf_op jit(solution)/shard_map/sum_all/pallas_call | solution.py:190
  82.6 3.3 %collective-permute-start.10 = (bf16[256,256]{1,0:T(8,128)(2,1)}, bf16[256,256]{1,0:T(8,128)(2,1)S(1)}, u32[]{:S(2)}, u32[]{:S(2)}) collective-permute-start(bf16[256,256]{1,0:T(8,128)(2,1)} %sum_all.3), channel_id=1, source_target_pairs={{0,96},{1,97},{2,98},{3,99},{4,100},{5,101},{6,102},{7,103},{8,104... | collective-permute-start | bytes 393224 | tf_op jit(solution)/shard_map/ppermute | solution.py:37
  87.0 6.9 %adam.2 = (f32[1024,512]{1,0:T(8,128)}, f32[1024,512]{1,0:T(8,128)}, f32[1024,512]{1,0:T(8,128)}) custom-call(s32[1,4096]{1,0:T(1,128)S(1)} %reshape.20.index_ref, s32[4,1,256]{2,1,0:T(1,128)S(1)} %bitcast.18, bf16[4096,256]{1,0:T(8,128)(2,1)} %bitcast.9.refs_0_, f32[1024,512]{1,0:T(8,128)} %refs_1_.3, f32[1024,512]{1,0:T(8,128)} %refs_2_.3, f32[1024,512]{1,0:T(8,128)} %refs_3_.3), custom_call_target="tpu_custom_call" | custom-call | tf_op jit(solution)/shard_map/adam/pallas_call | solution.py:271
  93.8 12.9 %collective-permute-done.10 = bf16[256,256]{1,0:T(8,128)(2,1)S(1)} collective-permute-done((bf16[256,256]{1,0:T(8,128)(2,1)}, bf16[256,256]{1,0:T(8,128)(2,1)S(1)}, u32[]{:S(2)}, u32[]{:S(2)}) %collective-permute-start.10) | collective-permute-done | bytes 131104 | tf_op jit(solution)/shard_map/ppermute | solution.py:37
  106.7 1.4 %collective-permute-done.12 = bf16[256,256]{1,0:T(8,128)(2,1)S(1)} collective-permute-done((bf16[256,256]{1,0:T(8,128)(2,1)}, bf16[256,256]{1,0:T(8,128)(2,1)S(1)}, u32[]{:S(2)}, u32[]{:S(2)}) %collective-permute-start.12) | collective-permute-done | bytes 131104 | tf_op jit(solution)/shard_map/ppermute | solution.py:37
  108.2 3.0 %collective-permute-start.13 = (bf16[4,256,256]{2,1,0:T(8,128)(2,1)S(1)}, bf16[4,256,256]{2,1,0:T(8,128)(2,1)S(1)}, u32[]{:S(2)}, u32[]{:S(2)}) collective-permute-start(bf16[4,256,256]{2,1,0:T(8,128)(2,1)S(1)} %pad_maximum_fusion.refs_0_), channel_id=1, source_target_pairs={{0,12},{1,13},{2,14},{3,15},{4,0},{5,1},{6,2},{7,3},{8,4},{9,5},{1... | collective-permute-start | bytes 1572872 | tf_op jit(solution)/shard_map/ppermute | solution.py:37
  112.8 6.0 %adam.3 = (f32[1024,512]{1,0:T(8,128)}, f32[1024,512]{1,0:T(8,128)}, f32[1024,512]{1,0:T(8,128)}) custom-call(s32[1,4096]{1,0:T(1,128)S(1)} %reshape.20.index_ref, s32[4,1,256]{2,1,0:T(1,128)S(1)} %bitcast.19, bf16[4096,256]{1,0:T(8,128)(2,1)S(1)} %bitcast.15, f32[1024,512]{1,0:T(8,128)} %refs_1_.3, ...), custom_call_target="tpu_custom_call", output_to_operand_aliasing={{0}: (6, {}), {1}: (7, {}), {2}: (8, {})} | custom-call | tf_op jit(solution)/shard_map/adam/pallas_call | solution.py:271
  118.8 4.1 %collective-permute-done.13.refs_1_ = bf16[4,256,256]{2,1,0:T(8,128)(2,1)S(1)} collective-permute-done((bf16[4,256,256]{2,1,0:T(8,128)(2,1)S(1)}, bf16[4,256,256]{2,1,0:T(8,128)(2,1)S(1)}, u32[]{:S(2)}, u32[]{:S(2)}) %collective-permute-start.13) | collective-permute-done | bytes 524320 | tf_op jit(solution)/shard_map/ppermute | solution.py:37
  122.9 3.8 %collective-permute-done.15.refs_3_ = bf16[4,256,256]{2,1,0:T(8,128)(2,1)} collective-permute-done((bf16[4,256,256]{2,1,0:T(8,128)(2,1)S(1)}, bf16[4,256,256]{2,1,0:T(8,128)(2,1)}, u32[]{:S(2)}, u32[]{:S(2)}) %collective-permute-start.15) | collective-permute-done | bytes 524320 | tf_op jit(solution)/shard_map/ppermute | solution.py:37
  126.7 0.9 collective-permute-start.17
  128.2 3.1 %place_half.2.refs_4_ = bf16[2,4096,256]{2,1,0:T(8,128)(2,1)} custom-call(s32[3]{0:T(128)S(1)} %pad_add_fusion.1.place_ref, bf16[4,256,256]{2,1,0:T(8,128)(2,1)S(1)} %pad_maximum_fusion.refs_0_, bf16[4,256,256]{2,1,0:T(8,128)(2,1)S(1)} %collective-permute-done.13.refs_1_, bf16[4,256,256]{2,1,0:T(8,128)(2,1)} %collective-permute-done.14.refs_2_, ...), custom_call_target="tpu_custom_call" | custom-call | tf_op jit(solution)/shard_map/place_half/pallas_call | solution.py:223
  131.4 3.1 %place_half.3 = bf16[2,4096,256]{2,1,0:T(8,128)(2,1)} custom-call(s32[3]{0:T(128)S(1)} %pad_add_fusion.place_ref, bf16[4,256,256]{2,1,0:T(8,128)(2,1)} %collective-permute-done.16.refs_0_, bf16[4,256,256]{2,1,0:T(8,128)(2,1)S(1)} %collective-permute-done.17.refs_1_, ...), custom_call_target="tpu_custom_call", output_to_operand_aliasing={{}: (5, {})} | custom-call | tf_op jit(solution)/shard_map/place_half/pallas_call | solution.py:223
  (57 shorter events, 6.7 us)
Async XLA Ops:
  0.8 2.2 %copy-start.1 = (bf16[256,2,4096]{2,1,0:T(2,128)(2,1)S(1)}, bf16[256,2,4096]{2,1,0:T(2,128)(2,1)}, u32[]{:S(2)}) copy-start(bf16[256,2,4096]{2,1,0:T(2,128)(2,1)} %score_ref.1) | copy-start | bytes 12582916
  3.0 7.0 %copy-start = (bf16[256,4096]{1,0:T(8,128)(2,1)S(1)}, bf16[256,4096]{1,0:T(8,128)(2,1)}, u32[]{:S(2)}) copy-start(bf16[256,4096]{1,0:T(8,128)(2,1)} %grad_ref.3) | copy-start | bytes 6291460
  3.0 7.0 %copy-start.3 = (s32[256,32]{0,1:T(8,128)S(1)}, s32[256,32]{0,1:T(8,128)}, u32[]{:S(2)}) copy-start(s32[256,32]{0,1:T(8,128)} %param.12) | copy-start | bytes 98308
  3.0 7.0 %copy-start.4 = (f32[256,32]{0,1:T(8,128)S(1)}, f32[256,32]{0,1:T(8,128)}, u32[]{:S(2)}) copy-start(f32[256,32]{0,1:T(8,128)} %param.11) | copy-start | bytes 98308
  8.5 7.5 %collective-permute-start = (bf16[4,4,256,256]{3,2,1,0:T(8,128)(2,1)S(1)}, bf16[4,4,256,256]{3,2,1,0:T(8,128)(2,1)S(1)}, u32[]{:S(2)}, u32[]{:S(2)}) collective-permute-start(bf16[4,4,256,256]{3,2,1,0:T(8,128)(2,1)S(1)} %get-tuple-element.45), channel_id=1, source_target_pairs={{0,16},{1,17},{2,18},{3,19},{4,20},{5,21},{6,22},{7,23},{8,24},{9,... | collective-permute-start | bytes 6291464 | tf_op jit(solution)/shard_map/ppermute | solution.py:37
  17.4 13.8 %collective-permute-start.1 = (bf16[4,256,256]{2,1,0:T(8,128)(2,1)}, bf16[4,256,256]{2,1,0:T(8,128)(2,1)S(1)}, u32[]{:S(2)}, u32[]{:S(2)}) collective-permute-start(bf16[4,256,256]{2,1,0:T(8,128)(2,1)} %get-tuple-element.51), channel_id=1, source_target_pairs={{0,32},{1,33},{2,34},{3,35},{4,36},{5,37},{6,38},{7,39},{8,40},{9,... | collective-permute-start | bytes 1572872 | tf_op jit(solution)/shard_map/ppermute | solution.py:37
  19.1 16.1 %collective-permute-start.2 = (bf16[4,256,256]{2,1,0:T(8,128)(2,1)}, bf16[4,256,256]{2,1,0:T(8,128)(2,1)}, u32[]{:S(2)}, u32[]{:S(2)}) collective-permute-start(bf16[4,256,256]{2,1,0:T(8,128)(2,1)} %get-tuple-element.52), channel_id=1, source_target_pairs={{0,64},{1,65},{2,66},{3,67},{4,68},{5,69},{6,70},{7,71},{8,72},{9,... | collective-permute-start | bytes 1572872 | tf_op jit(solution)/shard_map/ppermute | solution.py:37
  22.4 13.1 %collective-permute-start.3 = (bf16[4,256,256]{2,1,0:T(8,128)(2,1)}, bf16[4,256,256]{2,1,0:T(8,128)(2,1)}, u32[]{:S(2)}, u32[]{:S(2)}) collective-permute-start(bf16[4,256,256]{2,1,0:T(8,128)(2,1)} %get-tuple-element.53), channel_id=1, source_target_pairs={{0,96},{1,97},{2,98},{3,99},{4,100},{5,101},{6,102},{7,103},{8,104... | collective-permute-start | bytes 1572872 | tf_op jit(solution)/shard_map/ppermute | solution.py:37
  23.1 51.5 %all-to-all-start = ((bf16[128,32,256]{2,1,0:T(8,128)(2,1)}), bf16[128,32,256]{2,1,0:T(8,128)(2,1)}, u32[]{:S(2)}, u32[]{:S(2)}) async-start(bf16[128,32,256]{2,1,0:T(8,128)(2,1)} %get-tuple-element.59), calls=%async_computation | async-start | bytes 4194304 | tf_op jit(solution)/shard_map/all_to_all | solution.py:334
  31.2 18.3 %copy-start.2 = (bf16[512,256]{1,0:T(8,128)(2,1)S(1)}, bf16[512,256]{1,0:T(8,128)(2,1)}, u32[]{:S(2)}) copy-start(bf16[512,256]{1,0:T(8,128)(2,1)} %get-tuple-element.42.mix_ref) | copy-start | bytes 786436
  37.7 20.6 %collective-permute-start.4 = (bf16[256,256]{1,0:T(8,128)(2,1)}, bf16[256,256]{1,0:T(8,128)(2,1)S(1)}, u32[]{:S(2)}, u32[]{:S(2)}) collective-permute-start(bf16[256,256]{1,0:T(8,128)(2,1)} %get-tuple-element.55), channel_id=1, source_target_pairs={{0,4},{1,5},{2,6},{3,7},{4,8},{5,9},{6,10},{7,11},{8,12},{9,13},{1... | collective-permute-start | bytes 393224 | tf_op jit(solution)/shard_map/ppermute | solution.py:37
  45.0 14.7 %collective-permute-start.5 = (bf16[256,256]{1,0:T(8,128)(2,1)}, bf16[256,256]{1,0:T(8,128)(2,1)S(1)}, u32[]{:S(2)}, u32[]{:S(2)}) collective-permute-start(bf16[256,256]{1,0:T(8,128)(2,1)} %get-tuple-element.56), channel_id=1, source_target_pairs={{0,8},{1,9},{2,10},{3,11},{4,12},{5,13},{6,14},{7,15},{8,0},{9,1},... | collective-permute-start | bytes 393224 | tf_op jit(solution)/shard_map/ppermute | solution.py:37
  49.5 10.2 %collective-permute-start.6 = (bf16[256,256]{1,0:T(8,128)(2,1)}, bf16[256,256]{1,0:T(8,128)(2,1)S(1)}, u32[]{:S(2)}, u32[]{:S(2)}) collective-permute-start(bf16[256,256]{1,0:T(8,128)(2,1)} %get-tuple-element.57), channel_id=1, source_target_pairs={{0,12},{1,13},{2,14},{3,15},{4,0},{5,1},{6,2},{7,3},{8,4},{9,5},{1... | collective-permute-start | bytes 393224 | tf_op jit(solution)/shard_map/ppermute | solution.py:37
  58.3 1.4 %copy-start.6 = (bf16[256,256]{1,0:T(8,128)(2,1)}, bf16[256,256]{1,0:T(8,128)(2,1)S(1)}, u32[]{:S(2)}) copy-start(bf16[256,256]{1,0:T(8,128)(2,1)S(1)} %collective-permute-done.4.b_ref) | copy-start | bytes 393220
  59.7 0.7 copy-start.8
  62.2 17.2 %collective-permute-start.7 = (bf16[256,256]{1,0:T(8,128)(2,1)}, bf16[256,256]{1,0:T(8,128)(2,1)S(1)}, u32[]{:S(2)}, u32[]{:S(2)}) collective-permute-start(bf16[256,256]{1,0:T(8,128)(2,1)} %sum_all.2.a_ref), channel_id=1, source_target_pairs={{0,1},{1,2},{2,3},{3,0},{4,5},{5,6},{6,7},{7,4},{8,9},{9,10},{10,1... | collective-permute-start | bytes 393224 | tf_op jit(solution)/shard_map/ppermute | solution.py:37
  66.3 13.1 %collective-permute-start.8 = (bf16[256,256]{1,0:T(8,128)(2,1)}, bf16[256,256]{1,0:T(8,128)(2,1)S(1)}, u32[]{:S(2)}, u32[]{:S(2)}) collective-permute-start(bf16[256,256]{1,0:T(8,128)(2,1)} %sum_all.2.a_ref), channel_id=1, source_target_pairs={{0,2},{1,3},{2,0},{3,1},{4,6},{5,7},{6,4},{7,5},{8,10},{9,11},{10,... | collective-permute-start | bytes 393224 | tf_op jit(solution)/shard_map/ppermute | solution.py:37
  73.1 6.4 %collective-permute-start.9 = (bf16[256,256]{1,0:T(8,128)(2,1)}, bf16[256,256]{1,0:T(8,128)(2,1)S(1)}, u32[]{:S(2)}, u32[]{:S(2)}) collective-permute-start(bf16[256,256]{1,0:T(8,128)(2,1)} %sum_all.2.a_ref), channel_id=1, source_target_pairs={{0,3},{1,0},{2,1},{3,2},{4,7},{5,4},{6,5},{7,6},{8,11},{9,8},{10,9... | collective-permute-start | bytes 393224 | tf_op jit(solution)/shard_map/ppermute | solution.py:37
  74.6 38.2 %all-to-all-start.1 = ((bf16[128,32,256]{2,1,0:T(8,128)(2,1)}), bf16[128,32,256]{2,1,0:T(8,128)(2,1)S(1)}, u32[]{:S(2)}, u32[]{:S(2)}) async-start(bf16[128,32,256]{2,1,0:T(8,128)(2,1)} %combine_next.1), calls=%async_computation.1 | async-start | bytes 4194304 | tf_op jit(solution)/shard_map/all_to_all | solution.py:334
  79.4 7.3 %copy-start.10 = (s32[1,128,32]{1,2,0:T(8,128)S(1)}, s32[1,128,32]{1,2,0:T(8,128)}, u32[]{:S(2)}) copy-start(s32[1,128,32]{1,2,0:T(8,128)} %param.13) | copy-start | bytes 49156
  79.4 7.5 %copy-start.5 = (s32[1024]{0:T(1024)S(1)}, s32[1024]{0:T(1024)}, u32[]{:S(2)}) copy-start(s32[1024]{0:T(1024)} %param.17) | copy-start | bytes 12292
  82.6 24.1 %collective-permute-start.10 = (bf16[256,256]{1,0:T(8,128)(2,1)}, bf16[256,256]{1,0:T(8,128)(2,1)S(1)}, u32[]{:S(2)}, u32[]{:S(2)}) collective-permute-start(bf16[256,256]{1,0:T(8,128)(2,1)} %sum_all.3), channel_id=1, source_target_pairs={{0,96},{1,97},{2,98},{3,99},{4,100},{5,101},{6,102},{7,103},{8,104... | collective-permute-start | bytes 393224 | tf_op jit(solution)/shard_map/ppermute | solution.py:37
  85.9 20.8 %collective-permute-start.11 = (bf16[256,256]{1,0:T(8,128)(2,1)}, bf16[256,256]{1,0:T(8,128)(2,1)S(1)}, u32[]{:S(2)}, u32[]{:S(2)}) collective-permute-start(bf16[256,256]{1,0:T(8,128)(2,1)} %sum_all.3), channel_id=1, source_target_pairs={{0,64},{1,65},{2,66},{3,67},{4,68},{5,69},{6,70},{7,71},{8,72},{9,... | collective-permute-start | bytes 393224 | tf_op jit(solution)/shard_map/ppermute | solution.py:37
  85.9 22.2 %collective-permute-start.12 = (bf16[256,256]{1,0:T(8,128)(2,1)}, bf16[256,256]{1,0:T(8,128)(2,1)S(1)}, u32[]{:S(2)}, u32[]{:S(2)}) collective-permute-start(bf16[256,256]{1,0:T(8,128)(2,1)} %sum_all.3), channel_id=1, source_target_pairs={{0,32},{1,33},{2,34},{3,35},{4,36},{5,37},{6,38},{7,39},{8,40},{9,... | collective-permute-start | bytes 393224 | tf_op jit(solution)/shard_map/ppermute | solution.py:37
  87.0 21.1 %copy-start.9 = (bf16[256,256]{1,0:T(8,128)(2,1)S(1)}, bf16[256,256]{1,0:T(8,128)(2,1)}, u32[]{:S(2)}) copy-start(bf16[256,256]{1,0:T(8,128)(2,1)} %sum_all.3) | copy-start | bytes 393220
  108.2 14.7 %collective-permute-start.13 = (bf16[4,256,256]{2,1,0:T(8,128)(2,1)S(1)}, bf16[4,256,256]{2,1,0:T(8,128)(2,1)S(1)}, u32[]{:S(2)}, u32[]{:S(2)}) collective-permute-start(bf16[4,256,256]{2,1,0:T(8,128)(2,1)S(1)} %pad_maximum_fusion.refs_0_), channel_id=1, source_target_pairs={{0,12},{1,13},{2,14},{3,15},{4,0},{5,1},{6,2},{7,3},{8,4},{9,5},{1... | collective-permute-start | bytes 1572872 | tf_op jit(solution)/shard_map/ppermute | solution.py:37
  111.1 11.7 %collective-permute-start.14 = (bf16[4,256,256]{2,1,0:T(8,128)(2,1)S(1)}, bf16[4,256,256]{2,1,0:T(8,128)(2,1)}, u32[]{:S(2)}, u32[]{:S(2)}) collective-permute-start(bf16[4,256,256]{2,1,0:T(8,128)(2,1)S(1)} %pad_maximum_fusion.refs_0_), channel_id=1, source_target_pairs={{0,8},{1,9},{2,10},{3,11},{4,12},{5,13},{6,14},{7,15},{8,0},{9,1},... | collective-permute-start | bytes 1572872 | tf_op jit(solution)/shard_map/ppermute | solution.py:37
  111.7 15.0 %collective-permute-start.15 = (bf16[4,256,256]{2,1,0:T(8,128)(2,1)S(1)}, bf16[4,256,256]{2,1,0:T(8,128)(2,1)}, u32[]{:S(2)}, u32[]{:S(2)}) collective-permute-start(bf16[4,256,256]{2,1,0:T(8,128)(2,1)S(1)} %pad_maximum_fusion.refs_0_), channel_id=1, source_target_pairs={{0,4},{1,5},{2,6},{3,7},{4,8},{5,9},{6,10},{7,11},{8,12},{9,13},{1... | collective-permute-start | bytes 1572872 | tf_op jit(solution)/shard_map/ppermute | solution.py:37
  112.2 19.2 %collective-permute-start.16 = (bf16[4,256,256]{2,1,0:T(8,128)(2,1)S(1)}, bf16[4,256,256]{2,1,0:T(8,128)(2,1)}, u32[]{:S(2)}, u32[]{:S(2)}) collective-permute-start(bf16[4,256,256]{2,1,0:T(8,128)(2,1)S(1)} %pad_maximum_fusion.refs_0_), channel_id=1, source_target_pairs={{0,16},{1,17},{2,18},{3,19},{4,20},{5,21},{6,22},{7,23},{8,24},{9,... | collective-permute-start | bytes 1572872 | tf_op jit(solution)/shard_map/ppermute | solution.py:37
  126.7 4.7 %collective-permute-start.17 = (bf16[4,256,256]{2,1,0:T(8,128)(2,1)S(1)}, bf16[4,256,256]{2,1,0:T(8,128)(2,1)S(1)}, u32[]{:S(2)}, u32[]{:S(2)}) collective-permute-start(bf16[4,256,256]{2,1,0:T(8,128)(2,1)S(1)} %collective-permute-done.13.refs_1_), channel_id=1, source_target_pairs={{0,16},{1,17},{2,18},{3,19},{4,20},{5,21},{6,22},{7,23},{8,24},{9,... | collective-permute-start | bytes 1572872 | tf_op jit(solution)/shard_map/ppermute | solution.py:37
  127.6 3.8 %collective-permute-start.18 = (bf16[4,256,256]{2,1,0:T(8,128)(2,1)}, bf16[4,256,256]{2,1,0:T(8,128)(2,1)S(1)}, u32[]{:S(2)}, u32[]{:S(2)}) collective-permute-start(bf16[4,256,256]{2,1,0:T(8,128)(2,1)} %collective-permute-done.14.refs_2_), channel_id=1, source_target_pairs={{0,16},{1,17},{2,18},{3,19},{4,20},{5,21},{6,22},{7,23},{8,24},{9,... | collective-permute-start | bytes 1572872 | tf_op jit(solution)/shard_map/ppermute | solution.py:37
  127.6 3.8 %collective-permute-start.19 = (bf16[4,256,256]{2,1,0:T(8,128)(2,1)}, bf16[4,256,256]{2,1,0:T(8,128)(2,1)S(1)}, u32[]{:S(2)}, u32[]{:S(2)}) collective-permute-start(bf16[4,256,256]{2,1,0:T(8,128)(2,1)} %collective-permute-done.15.refs_3_), channel_id=1, source_target_pairs={{0,16},{1,17},{2,18},{3,19},{4,20},{5,21},{6,22},{7,23},{8,24},{9,... | collective-permute-start | bytes 1572872 | tf_op jit(solution)/shard_map/ppermute | solution.py:37
  (4 other events, 2.6 us)

commit v3 on v2

--- a/solution.py
+++ b/solution.py
@@ -6,7 +6,7 @@
 from jax.sharding import PartitionSpec as P
 
 AXES = ("dp", "table")
-ROLES = (("x", "y", "z"), ("z", "x", "y"))
+ROLES = (("x", "y", "z"), ("y", "z", "x"))
 BF = jnp.bfloat16
 F32 = jnp.float32
 
@@ -44,7 +44,7 @@
 BESIDE_TRANSFER = pl.CostEstimate(flops=10**11, bytes_accessed=0, transcendentals=0)
 
 
-def first_kernel(pos_ref, weight_ref, grad_ref, out_ref, mix_ref):
+def first_kernel(pos_ref, weight_ref, low_ref, high_ref, out_ref, mix_ref):
     slots, tokens = pos_ref.shape
     rows = mix_ref.shape[0]
     step = 64
@@ -63,50 +63,49 @@
 
         lax.fori_loop(0, rows // step, block, 0)
 
-    product = jnp.dot(mix_ref[...], grad_ref[...], preferred_element_type=F32)
-    out_ref[...] = product.astype(BF).reshape(out_ref.shape)
-
-
-def next_kernel(mix_ref, grad_ref, out_ref):
-    product = jnp.dot(mix_ref[...], grad_ref[...], preferred_element_type=F32)
-    out_ref[...] = product.astype(BF).reshape(out_ref.shape)
-
-
-def combine(slot_pos, slot_weight, grad_out, n_data, n_table, cap, pieces):
+    next_kernel(None, mix_ref, low_ref, high_ref, out_ref)
+
+
+def next_kernel(after_ref, mix_ref, low_ref, high_ref, out_ref):
+    half = out_ref.shape[0] // 2
+    for k, grad_ref in enumerate((low_ref, high_ref)):
+        product = jnp.dot(mix_ref[...], grad_ref[...], preferred_element_type=F32)
+        out_ref[k * half : (k + 1) * half] = product.astype(BF).reshape(half, *out_ref.shape[1:])
+
+
+def combine(after, slot_pos, slot_weight, grad_out, mix, n_data, n_table, cap, start, w):
     tokens, width = grad_out.shape
     rows = n_table * cap
-    columns = width // n_data // pieces
+    blocks = width // n_data // w
     slots = pl.BlockSpec((slot_pos.shape[1], tokens), lambda i: (0, 0))
     mixed = pl.BlockSpec((rows, tokens), lambda i: (0, 0))
-    out_spec = pl.BlockSpec((n_table, cap, columns), lambda i: (i, 0, 0))
-    out_shape = pltpu.HBM((n_data * n_table, cap, columns), BF)
+    grads = [
+        pl.BlockSpec((tokens, w), lambda i, half=half: (0, (2 * i + half) * blocks + start // w))
+        for half in range(2)
+    ]
+    out_spec = pl.BlockSpec((2 * n_table, cap, w), lambda i: (i, 0, 0))
+    out_shape = pltpu.HBM((n_data * n_table, cap, w), BF)
     params = pltpu.CompilerParams(vmem_limit_bytes=32 << 20)
-
-    def grad(k):
-        return pl.BlockSpec((tokens, columns), lambda i: (0, i * pieces + k))
-
-    first, mix = pl.pallas_call(
-        first_kernel,
-        grid=(n_data,),
-        in_specs=[slots, slots, grad(0)],
-        out_specs=[out_spec, mixed],
-        out_shape=[out_shape, pltpu.HBM((rows, tokens), BF)],
+    anywhere = pl.BlockSpec(memory_space=pl.ANY)
+    if mix is None:
+        return pl.pallas_call(
+            first_kernel,
+            grid=(n_data // 2,),
+            in_specs=[slots, slots, *grads],
+            out_specs=[out_spec, mixed],
+            out_shape=[out_shape, pltpu.HBM((rows, tokens), BF)],
+            compiler_params=params,
+            name="combine_first",
+        )(slot_pos.T, slot_weight.T, grad_out, grad_out)
+    return pl.pallas_call(
+        next_kernel,
+        grid=(n_data // 2,),
+        in_specs=[anywhere, mixed, *grads],
+        out_specs=out_spec,
+        out_shape=out_shape,
         compiler_params=params,
-        name="combine_first",
-    )(slot_pos.T, slot_weight.T, grad_out)
-    rest = [
-        pl.pallas_call(
-            next_kernel,
-            grid=(n_data,),
-            in_specs=[mixed, grad(k)],
-            out_specs=out_spec,
-            out_shape=out_shape,
-            compiler_params=params,
-            name="combine_next",
-        )(mix, grad_out)
-        for k in range(1, pieces)
-    ]
-    return [first, *rest]
+        name="combine_next",
+    )(after, mix, grad_out, grad_out)
 
 
 def partials_kernel(place_ref, score_ref, query_ref, own_ref, other_ref):
@@ -118,28 +117,27 @@
     product = lax.dot_general(
         score, both, (((0,), (0,)), ((), ())), preferred_element_type=F32
     ).astype(BF)
-    for j in range(4):
-        rows = product[j * 256 : (j + 1) * 256]
-        own_ref[0, (j - place_ref[2] + 4) % 4] = rows[:, :256]
-        other_ref[0, (j - place_ref[5] + 4) % 4] = rows[:, 256:]
+    own_ref[0] = product[:, : own_ref.shape[2]]
+    other_ref[0] = product[:, own_ref.shape[2] :]
 
 
 def partials(places, score, query):
     tokens, halves, keys = score.shape
     depth = query.shape[2]
-    shape = jax.ShapeDtypeStruct((4, 4, 256, depth), BF)
+    rows = keys // 4
+    shape = jax.ShapeDtypeStruct((4, rows, depth), BF)
     return pl.pallas_call(
         partials_kernel,
         grid_spec=pltpu.PrefetchScalarGridSpec(
             num_scalar_prefetch=1,
             grid=(4,),
             in_specs=[
-                pl.BlockSpec((tokens, halves, keys // 4), lambda i, p: (0, 0, i)),
+                pl.BlockSpec((tokens, halves, rows), lambda i, p: (0, 0, i)),
                 pl.BlockSpec((tokens, halves, depth), lambda i, p: (0, 0, 0)),
             ],
             out_specs=[
-                pl.BlockSpec((1, 4, 256, depth), lambda i, p: ((i - p[1] + 4) % 4, 0, 0, 0)),
-                pl.BlockSpec((1, 4, 256, depth), lambda i, p: ((i - p[4] + 4) % 4, 0, 0, 0)),
+                pl.BlockSpec((1, rows, depth), lambda i, p: ((i - p[1] + 4) % 4, 0, 0)),
+                pl.BlockSpec((1, rows, depth), lambda i, p: ((i - p[3] + 4) % 4, 0, 0)),
             ],
         ),
         out_shape=[shape] * 2,
@@ -162,59 +160,43 @@
     )(own, got)
 
 
-def sum_kernel(a_ref, b_ref, c_ref, d_ref, *out_refs):
-    for r, out_ref in enumerate(out_refs):
-        near = a_ref[r].astype(F32) + c_ref[r].astype(F32)
-        far = b_ref[r].astype(F32) + d_ref[r].astype(F32)
-        out_ref[...] = (near + far).astype(BF)
-
-
-def sum_chunks(chunks, cost=None):
-    shape = pltpu.HBM(chunks[0].shape[1:], BF)
+def sum_kernel(a_ref, b_ref, c_ref, d_ref, out_ref):
+    near = a_ref[...].astype(F32) + c_ref[...].astype(F32)
+    far = b_ref[...].astype(F32) + d_ref[...].astype(F32)
+    out_ref[...] = (near + far).astype(BF)
+
+
+def sum_chunks(chunks):
     return pl.pallas_call(
         sum_kernel,
-        out_shape=[shape] * 4,
-        cost_estimate=cost,
+        out_shape=pltpu.HBM(chunks[0].shape, BF),
+        cost_estimate=BESIDE_TRANSFER,
         compiler_params=pltpu.CompilerParams(vmem_limit_bytes=32 << 20),
         name="sum_chunks",
     )(*chunks)
 
 
-def sum_all_kernel(a_ref, b_ref, c_ref, d_ref, out_ref):
-    near = a_ref[...].astype(F32) + c_ref[...].astype(F32)
-    far = b_ref[...].astype(F32) + d_ref[...].astype(F32)
-    out_ref[...] = (near + far).astype(BF)
-
-
-def sum_all(chunks, cost=None):
-    return pl.pallas_call(
-        sum_all_kernel,
-        out_shape=jax.ShapeDtypeStruct(chunks[0].shape, BF),
-        cost_estimate=cost,
-        name="sum_all",
-    )(*chunks)
+def add_four(chunks):
+    near = chunks[0].astype(F32) + chunks[2].astype(F32)
+    return (near + (chunks[1].astype(F32) + chunks[3].astype(F32))).astype(BF)
 
 
 def place_kernel(place_ref, *refs):
     blocks = refs[:4]
     out_ref, held, sem_in, sem_out = refs[-4:]
+    rows = held.shape[1]
     loads = [pltpu.make_async_copy(blocks[k], held.at[k], sem_in.at[k]) for k in range(4)]
     for load in loads:
         load.start()
     stores = []
-    for rb in range(4):
-        loads[rb].wait()
-        for ra in range(4):
-            a = (place_ref[1] + ra) % 4
-            b = (place_ref[2] + rb) % 4
-            start = pl.multiple_of((a * 4 + b) * 256, 256)
-            store = pltpu.make_async_copy(
-                held.at[rb, ra],
-                out_ref.at[place_ref[0], pl.ds(start, 256)],
-                sem_out.at[rb * 4 + ra],
-            )
-            store.start()
-            stores.append(store)
+    for k in range(4):
+        loads[k].wait()
+        start = pl.multiple_of((place_ref[1] + k) % 4 * rows, rows)
+        store = pltpu.make_async_copy(
+            held.at[k], out_ref.at[place_ref[0], pl.ds(start, rows)], sem_out.at[k]
+        )
+        store.start()
+        stores.append(store)
     for store in stores:
         store.wait()
 
@@ -230,7 +212,7 @@
         scratch_shapes=[
             pltpu.VMEM((4, *buffers[0].shape), BF),
             pltpu.SemaphoreType.DMA((4,)),
-            pltpu.SemaphoreType.DMA((16,)),
+            pltpu.SemaphoreType.DMA((4,)),
         ],
         compiler_params=pltpu.CompilerParams(vmem_limit_bytes=16 << 20),
         name="place_half",
@@ -307,9 +289,7 @@
     core = dp % 2
     rows = []
     for c in (core, 1 - core):
-        a = jnp.where(c == 0, at[ROLES[0][0]], at[ROLES[1][0]])
-        b = jnp.where(c == 0, at[ROLES[0][1]], at[ROLES[1][1]])
-        rows += [c, a, b]
+        rows += [c, jnp.where(c == 0, at[ROLES[0][0]], at[ROLES[1][0]])]
     return jnp.stack(rows).astype(jnp.int32)
 
 
@@ -336,32 +316,30 @@
 
     own, other = partials(places, score_grad, queries)
     got = send(other, SWAP)
-    ordered = combine(slot_pos, slot_weight, grad_out, n_data, n_table, cap, 2)
+    sizes = (n_data, n_table, cap)
+    ordered, mix = combine(None, slot_pos, slot_weight, grad_out, None, *sizes, 0, 256)
     chunks = merge(own, got)
-    ordered[0], chunks = lax.optimization_barrier((ordered[0], chunks))
+    ordered, chunks = lax.optimization_barrier((ordered, chunks))
     chunks = [chunks[0]] + [send(chunks[r], ring(0, r)) for r in (1, 2, 3)]
-    arrived = [exchange(ordered[0])]
-    parts = sum_chunks(chunks, BESIDE_TRANSFER)
-    parts = [parts[0]] + [send(parts[r], ring(1, r)) for r in (1, 2, 3)]
-    total = sum_all(parts)
-    ordered[1], total = lax.optimization_barrier((ordered[1], total))
+    arrived = [exchange(ordered)]
+    total = sum_chunks(chunks)
+    total = add_four([total] + [send(total, ring(1, r)) for r in (1, 2, 3)])
+    ordered = combine(total, slot_pos, slot_weight, grad_out, mix, *sizes, 256, 256)
     around = [total] + [send(total, ring(2, r)) for r in (1, 2, 3)]
-    arrived.append(exchange(ordered[1]))
-    final = sum_all(around, BESIDE_TRANSFER)
-    mine = [final] + [send(final, ring(0, -r)) for r in (1, 2, 3)]
+    arrived.append(exchange(ordered))
 
     index = slot_rows.reshape(1, -1)
     steps = row_steps.reshape(-1, 1, 256)
     state = (values, first_moment, second_moment)
     outs = adam(index, steps, arrived[:1], state, 0)
-    mine, outs = lax.optimization_barrier((mine, outs))
-    mine = jnp.stack(mine)
-    buffers = [mine] + [send(mine, ring(1, -r)) for r in (1, 2, 3)]
+    around, outs = lax.optimization_barrier((around, outs))
+    final = sum_chunks(around)
+    buffers = [final] + [send(final, ring(0, -r)) for r in (1, 2, 3)]
     outs = adam(index, steps, arrived[1:], state, 1, outs)
     buffers[1:], outs = lax.optimization_barrier((buffers[1:], outs))
     theirs = [send(b, SWAP) for b in buffers]
-    subkey_out = place_half(places[:3], buffers)
-    subkey_out = place_half(places[3:], theirs, (subkey_out,))
+    subkey_out = place_half(places[:2], buffers)
+    subkey_out = place_half(places[2:], theirs, (subkey_out,))
     return (*outs, subkey_out)
 
 

time: 135 us -> 128 us (0.948)
  starting transfers between devices: 54.5 us -> 43.5 us
  waiting for transfers between devices: 32.7 us -> 41.5 us
  Pallas kernels: 41.7 us -> 37.6 us
  local copies, waits for them, and re-layouts: 4.52 us -> 2.41 us
    all_to_all x2, waiting for transfers between devices: 0.01 us -> 15.3 us  [exchange(): lax.all_to_all(ordered, AXES, split_axis=0, concat_axis=0, tiled=True)]
    ppermute x20 -> x17, starting transfers between devices: 41.7 us -> 29.2 us  [send(): return lax.ppermute(value, AXES, pairs)]
    ppermute x20 -> x17, waiting for transfers between devices: 32.6 us -> 26.2 us  [send(): return lax.ppermute(value, AXES, pairs)]
    pallas_call x5 -> x4, Pallas kernels: 15.8 us -> 12 us  [the longest x2 4.81 us: sum_chunks(): pl.pallas_call(sum_kernel, out_shape=pltpu.HBM(chunks[0].shape, BF), cost...]
    unnamed x29 -> x17, local copies, waits for them, and re-layouts: 4.34 us -> 2.31 us
    all_to_all x2, starting transfers between devices: 12.8 us -> 14.3 us  [exchange(): lax.all_to_all(ordered, AXES, split_axis=0, concat_axis=0, tiled=True)]
  transfers between devices with their start and end apart: 22 -> 19, of which waited for: 8 -> 7; matrix products, arithmetic and copies ran while one was open for 0% -> 1% of each run, Pallas kernels for 24% -> 22%
where the time goes in v3:
time: 128 us; the launch traced here: 127 us
  starting transfers between devices  43.5 us (34%)
  waiting for transfers between devices  41.5 us (32%)
  Pallas kernels  37.6 us (29%)
  local copies, waits for them, and re-layouts  2.41 us (2%)
  other arithmetic  1.52 us (1%)
    ppermute x17, starting transfers between devices, send(): return lax.ppermute(value, AXES, pairs)  29.2 us
    ppermute x17, waiting for transfers between devices, send(): return lax.ppermute(value, AXES, pairs)  26.2 us
    all_to_all x2, waiting for transfers between devices, exchange(): lax.all_to_all(ordered, AXES, split_axis=0, concat_axis=0, tiled=True)  15.3 us
    all_to_all x2, starting transfers between devices, exchange(): lax.all_to_all(ordered, AXES, split_axis=0, concat_axis=0, tiled=True)  14.3 us
    pallas_call x2, Pallas kernels, adam(): pl.pallas_call(adam_kernel, grid=(owned // rows,), in_specs=[pl.BlockSpec...  12.9 us
    pallas_call x2, Pallas kernels, place_half(): pl.pallas_call(place_kernel, in_specs=[pl.BlockSpec(memory_space=pltpu.SM...  5.85 us
    pallas_call x1, Pallas kernels, partials(): pl.pallas_call(partials_kernel, grid_spec=pltpu.PrefetchScalarGridSpec(nu...  5.53 us
    pallas_call x2, Pallas kernels, sum_chunks(): pl.pallas_call(sum_kernel, out_shape=pltpu.HBM(chunks[0].shape, BF), cost...  4.81 us
  transfers between devices with their start and end apart: 19, of which 7 were waited for; matrix products, arithmetic and copies ran while one was open for 1% of the time, Pallas kernels for 22%

profile of v3, /device:TPU:1, one launch (start us, length us, event | category | flops | bytes accessed | tf_op | source)
XLA Modules:
  0.0 127.4 jit_solution(5475096169528201427)
XLA Ops:
  0.8 2.2 %copy-done.1 = bf16[256,2,4096]{2,1,0:T(2,128)(2,1)S(1)} copy-done((bf16[256,2,4096]{2,1,0:T(2,128)(2,1)S(1)}, bf16[256,2,4096]{2,1,0:T(2,128)(2,1)}, u32[]{:S(2)}) %copy-start.1) | copy-done | bytes 4194328
  2.9 5.5 %partials.1 = (bf16[4,1024,256]{2,1,0:T(8,128)(2,1)S(1)}, bf16[4,1024,256]{2,1,0:T(8,128)(2,1)S(1)}) custom-call(s32[4]{0:T(128)S(1)} %pad_add_fusion.place_ref, bf16[256,2,4096]{2,1,0:T(2,128)(2,1)S(1)} %copy-done.1, bf16[256,2,256]{2,1,0:T(2,128)(2,1)} %query_ref.1), custom_call_target="tpu_custom_call" | custom-call | tf_op jit(solution)/shard_map/partials/pallas_call | solution.py:129
  8.5 1.5 %collective-permute-start = (bf16[4,1024,256]{2,1,0:T(8,128)(2,1)S(1)}, bf16[4,1024,256]{2,1,0:T(8,128)(2,1)S(1)}, u32[]{:S(2)}, u32[]{:S(2)}) collective-permute-start(bf16[4,1024,256]{2,1,0:T(8,128)(2,1)S(1)} %get-tuple-element.38), channel_id=1, source_target_pairs={{0,16},{1,17},{2,18},{3,19},{4,20},{5,21},{6,22},{7,23},{8,24},{9,... | collective-permute-start | bytes 6291464 | tf_op jit(solution)/shard_map/ppermute | solution.py:37
  10.0 4.6 %combine_first.1 = (bf16[128,32,256]{2,1,0:T(8,128)(2,1)}, bf16[512,256]{1,0:T(8,128)(2,1)}) custom-call(s32[32,256]{1,0:T(8,128)S(1)} %bitcast.10, f32[32,256]{1,0:T(8,128)S(1)} %bitcast.11, bf16[256,4096]{1,0:T(8,128)(2,1)S(1)} %copy-done, bf16[256,4096]{1,0:T(8,128)(2,1)S(1)} %copy-done), custom_call_target="tpu_custom_call" | custom-call | tf_op jit(solution)/shard_map/combine_first/pallas_call | solution.py:91
  14.6 1.4 %merge.1 = (bf16[1024,256]{1,0:T(8,128)(2,1)S(1)}, bf16[1024,256]{1,0:T(8,128)(2,1)}, bf16[1024,256]{1,0:T(8,128)(2,1)}, bf16[1024,256]{1,0:T(8,128)(2,1)S(1)}) custom-call(bf16[4,1024,256]{2,1,0:T(8,128)(2,1)S(1)} %get-tuple-element.37.own_ref, bf16[4,1024,256]{2,1,0:T(8,128)(2,1)S(1)} %collective-permute-done.got_ref), custom_call_target="tpu_custom_call" | custom-call | tf_op jit(solution)/shard_map/merge/pallas_call | solution.py:155
  15.9 1.4 %collective-permute-start.1 = (bf16[1024,256]{1,0:T(8,128)(2,1)}, bf16[1024,256]{1,0:T(8,128)(2,1)}, u32[]{:S(2)}, u32[]{:S(2)}) collective-permute-start(bf16[1024,256]{1,0:T(8,128)(2,1)} %get-tuple-element.44), channel_id=1, source_target_pairs={{0,32},{1,33},{2,34},{3,35},{4,36},{5,37},{6,38},{7,39},{8,40},{9,... | collective-permute-start | bytes 1572872 | tf_op jit(solution)/shard_map/ppermute | solution.py:37
  17.3 2.6 %collective-permute-start.2 = (bf16[1024,256]{1,0:T(8,128)(2,1)}, bf16[1024,256]{1,0:T(8,128)(2,1)}, u32[]{:S(2)}, u32[]{:S(2)}) collective-permute-start(bf16[1024,256]{1,0:T(8,128)(2,1)} %get-tuple-element.45), channel_id=1, source_target_pairs={{0,64},{1,65},{2,66},{3,67},{4,68},{5,69},{6,70},{7,71},{8,72},{9,... | collective-permute-start | bytes 1572872 | tf_op jit(solution)/shard_map/ppermute | solution.py:37
  19.9 1.1 collective-permute-start.3
  21.0 8.7 %all-to-all-start = ((bf16[128,32,256]{2,1,0:T(8,128)(2,1)}), bf16[128,32,256]{2,1,0:T(8,128)(2,1)}, u32[]{:S(2)}, u32[]{:S(2)}) async-start(bf16[128,32,256]{2,1,0:T(8,128)(2,1)} %get-tuple-element.47), calls=%async_computation | async-start | bytes 4194304 | tf_op jit(solution)/shard_map/all_to_all | solution.py:314
  29.8 3.0 %collective-permute-done.2.c_ref = bf16[1024,256]{1,0:T(8,128)(2,1)} collective-permute-done((bf16[1024,256]{1,0:T(8,128)(2,1)}, bf16[1024,256]{1,0:T(8,128)(2,1)}, u32[]{:S(2)}, u32[]{:S(2)}) %collective-permute-start.2) | collective-permute-done | bytes 524320 | tf_op jit(solution)/shard_map/ppermute | solution.py:37
  33.4 2.4 %sum_chunks.2 = bf16[1024,256]{1,0:T(8,128)(2,1)} custom-call(bf16[1024,256]{1,0:T(8,128)(2,1)S(1)} %get-tuple-element.43.a_ref, bf16[1024,256]{1,0:T(8,128)(2,1)} %collective-permute-done.1.b_ref, bf16[1024,256]{1,0:T(8,128)(2,1)} %collective-permute-done.2.c_ref, bf16[1024,256]{1,0:T(8,128)(2,1)} %collective-permute-done.3.d_ref), custom_call_target="tpu_custom_call" | custom-call | flops 99999997952 | tf_op jit(solution)/shard_map/sum_chunks/pallas_call | solution.py:170
  35.8 8.0 %collective-permute-start.6 = (bf16[1024,256]{1,0:T(8,128)(2,1)}, bf16[1024,256]{1,0:T(8,128)(2,1)S(1)}, u32[]{:S(2)}, u32[]{:S(2)}) collective-permute-start(bf16[1024,256]{1,0:T(8,128)(2,1)} %sum_chunks.2), channel_id=1, source_target_pairs={{0,12},{1,13},{2,14},{3,15},{4,0},{5,1},{6,2},{7,3},{8,4},{9,5},{1... | collective-permute-start | bytes 1572872 | tf_op jit(solution)/shard_map/ppermute | solution.py:37
  43.8 2.1 %collective-permute-start.5 = (bf16[1024,256]{1,0:T(8,128)(2,1)}, bf16[1024,256]{1,0:T(8,128)(2,1)S(1)}, u32[]{:S(2)}, u32[]{:S(2)}) collective-permute-start(bf16[1024,256]{1,0:T(8,128)(2,1)} %sum_chunks.2), channel_id=1, source_target_pairs={{0,4},{1,5},{2,6},{3,7},{4,8},{5,9},{6,10},{7,11},{8,12},{9,13},{1... | collective-permute-start | bytes 1572872 | tf_op jit(solution)/shard_map/ppermute | solution.py:37
  45.9 1.7 %collective-permute-start.4 = (bf16[1024,256]{1,0:T(8,128)(2,1)}, bf16[1024,256]{1,0:T(8,128)(2,1)S(1)}, u32[]{:S(2)}, u32[]{:S(2)}) collective-permute-start(bf16[1024,256]{1,0:T(8,128)(2,1)} %sum_chunks.2), channel_id=1, source_target_pairs={{0,8},{1,9},{2,10},{3,11},{4,12},{5,13},{6,14},{7,15},{8,0},{9,1},... | collective-permute-start | bytes 1572872 | tf_op jit(solution)/shard_map/ppermute | solution.py:37
  47.6 13.9 %collective-permute-done.6 = bf16[1024,256]{1,0:T(8,128)(2,1)S(1)} collective-permute-done((bf16[1024,256]{1,0:T(8,128)(2,1)}, bf16[1024,256]{1,0:T(8,128)(2,1)S(1)}, u32[]{:S(2)}, u32[]{:S(2)}) %collective-permute-start.6) | collective-permute-done | bytes 524320 | tf_op jit(solution)/shard_map/ppermute | solution.py:37
  61.5 1.5 %collective-permute-done.5 = bf16[1024,256]{1,0:T(8,128)(2,1)S(1)} collective-permute-done((bf16[1024,256]{1,0:T(8,128)(2,1)}, bf16[1024,256]{1,0:T(8,128)(2,1)S(1)}, u32[]{:S(2)}, u32[]{:S(2)}) %collective-permute-start.5) | collective-permute-done | bytes 524320 | tf_op jit(solution)/shard_map/ppermute | solution.py:37
  63.0 5.6 %collective-permute-done.4 = bf16[1024,256]{1,0:T(8,128)(2,1)S(1)} collective-permute-done((bf16[1024,256]{1,0:T(8,128)(2,1)}, bf16[1024,256]{1,0:T(8,128)(2,1)S(1)}, u32[]{:S(2)}, u32[]{:S(2)}) %collective-permute-start.4) | collective-permute-done | bytes 524320 | tf_op jit(solution)/shard_map/ppermute | solution.py:37
  68.6 1.3 %add_convert_fusion.a_ref.after_ref = bf16[1024,256]{1,0:T(8,128)(2,1)S(1)} fusion(bf16[1024,256]{1,0:T(8,128)(2,1)S(1)} %collective-permute-done.6, bf16[1024,256]{1,0:T(8,128)(2,1)S(1)} %collective-permute-done.5, bf16[1024,256]{1,0:T(8,128)(2,1)S(1)} %collective-permute-done.4, bf16[1024,256]{1,0:T(8,128)(2,1)} %sum_chunks.2), kind=kLoop, calls=%fused_computation | loop fusion | flops 2097152 | bytes 2621440 | tf_op jit(solution)/shard_map/convert_element_type | solution.py:181
  69.9 1.2 collective-permute-start.7
  71.1 3.0 %collective-permute-start.8 = (bf16[1024,256]{1,0:T(8,128)(2,1)S(1)}, bf16[1024,256]{1,0:T(8,128)(2,1)}, u32[]{:S(2)}, u32[]{:S(2)}) collective-permute-start(bf16[1024,256]{1,0:T(8,128)(2,1)S(1)} %add_convert_fusion.a_ref.after_ref), channel_id=1, source_target_pairs={{0,2},{1,3},{2,0},{3,1},{4,6},{5,7},{6,4},{7,5},{8,10},{9,11},{10,... | collective-permute-start | bytes 1572872 | tf_op jit(solution)/shard_map/ppermute | solution.py:37
  74.1 0.8 collective-permute-start.9
  75.1 2.6 %combine_next.1 = bf16[128,32,256]{2,1,0:T(8,128)(2,1)} custom-call(bf16[1024,256]{1,0:T(8,128)(2,1)S(1)} %add_convert_fusion.a_ref.after_ref, bf16[512,256]{1,0:T(8,128)(2,1)S(1)} %copy-done.3, bf16[256,4096]{1,0:T(8,128)(2,1)S(1)} %copy-done, bf16[256,4096]{1,0:T(8,128)(2,1)S(1)} %copy-done), custom_call_target="tpu_custom_call" | custom-call | tf_op jit(solution)/shard_map/combine_next/pallas_call | solution.py:100
  77.8 5.6 %all-to-all-start.1 = ((bf16[128,32,256]{2,1,0:T(8,128)(2,1)}), bf16[128,32,256]{2,1,0:T(8,128)(2,1)S(1)}, u32[]{:S(2)}, u32[]{:S(2)}) async-start(bf16[128,32,256]{2,1,0:T(8,128)(2,1)} %combine_next.1), calls=%async_computation.1 | async-start | bytes 4194304 | tf_op jit(solution)/shard_map/all_to_all | solution.py:314
  83.4 6.8 %adam.2 = (f32[1024,512]{1,0:T(8,128)}, f32[1024,512]{1,0:T(8,128)}, f32[1024,512]{1,0:T(8,128)}) custom-call(s32[1,4096]{1,0:T(1,128)S(1)} %reshape.20.index_ref, s32[4,1,256]{2,1,0:T(1,128)S(1)} %bitcast.12, bf16[4096,256]{1,0:T(8,128)(2,1)} %bitcast.7.refs_0_, f32[1024,512]{1,0:T(8,128)} %refs_1_.3, f32[1024,512]{1,0:T(8,128)} %refs_2_.3, f32[1024,512]{1,0:T(8,128)} %refs_3_.3), custom_call_target="tpu_custom_call" | custom-call | tf_op jit(solution)/shard_map/adam/pallas_call | solution.py:253
  90.2 2.4 %sum_chunks.3.refs_0_ = bf16[1024,256]{1,0:T(8,128)(2,1)} custom-call(bf16[1024,256]{1,0:T(8,128)(2,1)S(1)} %add_convert_fusion.a_ref.after_ref, bf16[1024,256]{1,0:T(8,128)(2,1)} %collective-permute-done.7.b_ref, bf16[1024,256]{1,0:T(8,128)(2,1)} %collective-permute-done.8.c_ref, bf16[1024,256]{1,0:T(8,128)(2,1)} %collective-permute-done.9.d_ref), custom_call_target="tpu_custom_call" | custom-call | flops 99999997952 | tf_op jit(solution)/shard_map/sum_chunks/pallas_call | solution.py:170
  92.6 2.6 %collective-permute-start.10 = (bf16[1024,256]{1,0:T(8,128)(2,1)}, bf16[1024,256]{1,0:T(8,128)(2,1)S(1)}, u32[]{:S(2)}, u32[]{:S(2)}) collective-permute-start(bf16[1024,256]{1,0:T(8,128)(2,1)} %sum_chunks.3.refs_0_), channel_id=1, source_target_pairs={{0,96},{1,97},{2,98},{3,99},{4,100},{5,101},{6,102},{7,103},{8,104... | collective-permute-start | bytes 1572872 | tf_op jit(solution)/shard_map/ppermute | solution.py:37
  96.4 1.2 collective-permute-start.13
  97.6 15.3 %all-to-all-done.1 = bf16[128,32,256]{2,1,0:T(8,128)(2,1)S(1)} async-done(((bf16[128,32,256]{2,1,0:T(8,128)(2,1)}), bf16[128,32,256]{2,1,0:T(8,128)(2,1)S(1)}, u32[]{:S(2)}, u32[]{:S(2)}) %all-to-all-start.1) | async-done | bytes 2097184 | tf_op jit(solution)/shard_map/all_to_all | solution.py:314
  112.9 6.0 %adam.3 = (f32[1024,512]{1,0:T(8,128)}, f32[1024,512]{1,0:T(8,128)}, f32[1024,512]{1,0:T(8,128)}) custom-call(s32[1,4096]{1,0:T(1,128)S(1)} %reshape.20.index_ref, s32[4,1,256]{2,1,0:T(1,128)S(1)} %bitcast.13, bf16[4096,256]{1,0:T(8,128)(2,1)S(1)} %bitcast.9, f32[1024,512]{1,0:T(8,128)} %refs_1_.3, ...), custom_call_target="tpu_custom_call", output_to_operand_aliasing={{0}: (6, {}), {1}: (7, {}), {2}: (8, {})} | custom-call | tf_op jit(solution)/shard_map/adam/pallas_call | solution.py:253
  119.0 1.4 %collective-permute-done.12.refs_3_ = bf16[1024,256]{1,0:T(8,128)(2,1)} collective-permute-done((bf16[1024,256]{1,0:T(8,128)(2,1)}, bf16[1024,256]{1,0:T(8,128)(2,1)}, u32[]{:S(2)}, u32[]{:S(2)}) %collective-permute-start.12) | collective-permute-done | bytes 524320 | tf_op jit(solution)/shard_map/ppermute | solution.py:37
  121.5 2.9 %place_half.2.refs_4_ = bf16[2,4096,256]{2,1,0:T(8,128)(2,1)} custom-call(s32[2]{0:T(128)S(1)} %pad_add_fusion.2.place_ref, bf16[1024,256]{1,0:T(8,128)(2,1)S(1)} %copy-done.2, bf16[1024,256]{1,0:T(8,128)(2,1)S(1)} %collective-permute-done.10.refs_1_, bf16[1024,256]{1,0:T(8,128)(2,1)S(1)} %collective-permute-done.11.refs_2_, ...), custom_call_target="tpu_custom_call" | custom-call | tf_op jit(solution)/shard_map/place_half/pallas_call | solution.py:205
  124.4 3.0 %place_half.3 = bf16[2,4096,256]{2,1,0:T(8,128)(2,1)} custom-call(s32[2]{0:T(128)S(1)} %pad_add_fusion.1.place_ref, bf16[1024,256]{1,0:T(8,128)(2,1)} %collective-permute-done.13.refs_0_, bf16[1024,256]{1,0:T(8,128)(2,1)S(1)} %collective-permute-done.14.refs_1_, ...), custom_call_target="tpu_custom_call", output_to_operand_aliasing={{}: (5, {})} | custom-call | tf_op jit(solution)/shard_map/place_half/pallas_call | solution.py:205
  (38 shorter events, 3.2 us)
Async XLA Ops:
  0.7 2.2 %copy-start.1 = (bf16[256,2,4096]{2,1,0:T(2,128)(2,1)S(1)}, bf16[256,2,4096]{2,1,0:T(2,128)(2,1)}, u32[]{:S(2)}) copy-start(bf16[256,2,4096]{2,1,0:T(2,128)(2,1)} %score_ref.1) | copy-start | bytes 12582916
  2.9 7.0 %copy-start = (bf16[256,4096]{1,0:T(8,128)(2,1)S(1)}, bf16[256,4096]{1,0:T(8,128)(2,1)}, u32[]{:S(2)}) copy-start(bf16[256,4096]{1,0:T(8,128)(2,1)} %high_ref.3) | copy-start | bytes 6291460
  2.9 7.0 %copy-start.4 = (s32[256,32]{0,1:T(8,128)S(1)}, s32[256,32]{0,1:T(8,128)}, u32[]{:S(2)}) copy-start(s32[256,32]{0,1:T(8,128)} %param.12) | copy-start | bytes 98308
  2.9 7.0 %copy-start.5 = (f32[256,32]{0,1:T(8,128)S(1)}, f32[256,32]{0,1:T(8,128)}, u32[]{:S(2)}) copy-start(f32[256,32]{0,1:T(8,128)} %param.11) | copy-start | bytes 98308
  8.5 6.1 %collective-permute-start = (bf16[4,1024,256]{2,1,0:T(8,128)(2,1)S(1)}, bf16[4,1024,256]{2,1,0:T(8,128)(2,1)S(1)}, u32[]{:S(2)}, u32[]{:S(2)}) collective-permute-start(bf16[4,1024,256]{2,1,0:T(8,128)(2,1)S(1)} %get-tuple-element.38), channel_id=1, source_target_pairs={{0,16},{1,17},{2,18},{3,19},{4,20},{5,21},{6,22},{7,23},{8,24},{9,... | collective-permute-start | bytes 6291464 | tf_op jit(solution)/shard_map/ppermute | solution.py:37
  15.9 13.8 %collective-permute-start.1 = (bf16[1024,256]{1,0:T(8,128)(2,1)}, bf16[1024,256]{1,0:T(8,128)(2,1)}, u32[]{:S(2)}, u32[]{:S(2)}) collective-permute-start(bf16[1024,256]{1,0:T(8,128)(2,1)} %get-tuple-element.44), channel_id=1, source_target_pairs={{0,32},{1,33},{2,34},{3,35},{4,36},{5,37},{6,38},{7,39},{8,40},{9,... | collective-permute-start | bytes 1572872 | tf_op jit(solution)/shard_map/ppermute | solution.py:37
  17.3 15.4 %collective-permute-start.2 = (bf16[1024,256]{1,0:T(8,128)(2,1)}, bf16[1024,256]{1,0:T(8,128)(2,1)}, u32[]{:S(2)}, u32[]{:S(2)}) collective-permute-start(bf16[1024,256]{1,0:T(8,128)(2,1)} %get-tuple-element.45), channel_id=1, source_target_pairs={{0,64},{1,65},{2,66},{3,67},{4,68},{5,69},{6,70},{7,71},{8,72},{9,... | collective-permute-start | bytes 1572872 | tf_op jit(solution)/shard_map/ppermute | solution.py:37
  19.9 13.5 %collective-permute-start.3 = (bf16[1024,256]{1,0:T(8,128)(2,1)S(1)}, bf16[1024,256]{1,0:T(8,128)(2,1)}, u32[]{:S(2)}, u32[]{:S(2)}) collective-permute-start(bf16[1024,256]{1,0:T(8,128)(2,1)S(1)} %get-tuple-element.46), channel_id=1, source_target_pairs={{0,96},{1,97},{2,98},{3,99},{4,100},{5,101},{6,102},{7,103},{8,104... | collective-permute-start | bytes 1572872 | tf_op jit(solution)/shard_map/ppermute | solution.py:37
  21.0 56.8 %all-to-all-start = ((bf16[128,32,256]{2,1,0:T(8,128)(2,1)}), bf16[128,32,256]{2,1,0:T(8,128)(2,1)}, u32[]{:S(2)}, u32[]{:S(2)}) async-start(bf16[128,32,256]{2,1,0:T(8,128)(2,1)} %get-tuple-element.47), calls=%async_computation | async-start | bytes 4194304 | tf_op jit(solution)/shard_map/all_to_all | solution.py:314
  35.8 39.1 %copy-start.7 = (s32[1,128,32]{1,2,0:T(8,128)S(1)}, s32[1,128,32]{1,2,0:T(8,128)}, u32[]{:S(2)}) copy-start(s32[1,128,32]{1,2,0:T(8,128)} %param.13) | copy-start | bytes 49156
  35.8 39.3 %copy-start.3 = (bf16[512,256]{1,0:T(8,128)(2,1)S(1)}, bf16[512,256]{1,0:T(8,128)(2,1)}, u32[]{:S(2)}) copy-start(bf16[512,256]{1,0:T(8,128)(2,1)} %get-tuple-element.55.mix_ref) | copy-start | bytes 786436
  35.8 25.7 %collective-permute-start.6 = (bf16[1024,256]{1,0:T(8,128)(2,1)}, bf16[1024,256]{1,0:T(8,128)(2,1)S(1)}, u32[]{:S(2)}, u32[]{:S(2)}) collective-permute-start(bf16[1024,256]{1,0:T(8,128)(2,1)} %sum_chunks.2), channel_id=1, source_target_pairs={{0,12},{1,13},{2,14},{3,15},{4,0},{5,1},{6,2},{7,3},{8,4},{9,5},{1... | collective-permute-start | bytes 1572872 | tf_op jit(solution)/shard_map/ppermute | solution.py:37
  43.8 19.2 %collective-permute-start.5 = (bf16[1024,256]{1,0:T(8,128)(2,1)}, bf16[1024,256]{1,0:T(8,128)(2,1)S(1)}, u32[]{:S(2)}, u32[]{:S(2)}) collective-permute-start(bf16[1024,256]{1,0:T(8,128)(2,1)} %sum_chunks.2), channel_id=1, source_target_pairs={{0,4},{1,5},{2,6},{3,7},{4,8},{5,9},{6,10},{7,11},{8,12},{9,13},{1... | collective-permute-start | bytes 1572872 | tf_op jit(solution)/shard_map/ppermute | solution.py:37
  45.9 22.8 %collective-permute-start.4 = (bf16[1024,256]{1,0:T(8,128)(2,1)}, bf16[1024,256]{1,0:T(8,128)(2,1)S(1)}, u32[]{:S(2)}, u32[]{:S(2)}) collective-permute-start(bf16[1024,256]{1,0:T(8,128)(2,1)} %sum_chunks.2), channel_id=1, source_target_pairs={{0,8},{1,9},{2,10},{3,11},{4,12},{5,13},{6,14},{7,15},{8,0},{9,1},... | collective-permute-start | bytes 1572872 | tf_op jit(solution)/shard_map/ppermute | solution.py:37
  69.9 20.3 %collective-permute-start.7 = (bf16[1024,256]{1,0:T(8,128)(2,1)S(1)}, bf16[1024,256]{1,0:T(8,128)(2,1)}, u32[]{:S(2)}, u32[]{:S(2)}) collective-permute-start(bf16[1024,256]{1,0:T(8,128)(2,1)S(1)} %add_convert_fusion.a_ref.after_ref), channel_id=1, source_target_pairs={{0,1},{1,2},{2,3},{3,0},{4,5},{5,6},{6,7},{7,4},{8,9},{9,10},{10,1... | collective-permute-start | bytes 1572872 | tf_op jit(solution)/shard_map/ppermute | solution.py:37
  71.1 19.1 %collective-permute-start.8 = (bf16[1024,256]{1,0:T(8,128)(2,1)S(1)}, bf16[1024,256]{1,0:T(8,128)(2,1)}, u32[]{:S(2)}, u32[]{:S(2)}) collective-permute-start(bf16[1024,256]{1,0:T(8,128)(2,1)S(1)} %add_convert_fusion.a_ref.after_ref), channel_id=1, source_target_pairs={{0,2},{1,3},{2,0},{3,1},{4,6},{5,7},{6,4},{7,5},{8,10},{9,11},{10,... | collective-permute-start | bytes 1572872 | tf_op jit(solution)/shard_map/ppermute | solution.py:37
  74.1 16.1 %collective-permute-start.9 = (bf16[1024,256]{1,0:T(8,128)(2,1)S(1)}, bf16[1024,256]{1,0:T(8,128)(2,1)}, u32[]{:S(2)}, u32[]{:S(2)}) collective-permute-start(bf16[1024,256]{1,0:T(8,128)(2,1)S(1)} %add_convert_fusion.a_ref.after_ref), channel_id=1, source_target_pairs={{0,3},{1,0},{2,1},{3,2},{4,7},{5,4},{6,5},{7,6},{8,11},{9,8},{10,9... | collective-permute-start | bytes 1572872 | tf_op jit(solution)/shard_map/ppermute | solution.py:37
  77.8 5.6 %copy-start.6 = (s32[1024]{0:T(1024)S(1)}, s32[1024]{0:T(1024)}, u32[]{:S(2)}) copy-start(s32[1024]{0:T(1024)} %param.17) | copy-start | bytes 12292
  77.8 35.2 %all-to-all-start.1 = ((bf16[128,32,256]{2,1,0:T(8,128)(2,1)}), bf16[128,32,256]{2,1,0:T(8,128)(2,1)S(1)}, u32[]{:S(2)}, u32[]{:S(2)}) async-start(bf16[128,32,256]{2,1,0:T(8,128)(2,1)} %combine_next.1), calls=%async_computation.1 | async-start | bytes 4194304 | tf_op jit(solution)/shard_map/all_to_all | solution.py:314
  92.6 26.3 %collective-permute-start.10 = (bf16[1024,256]{1,0:T(8,128)(2,1)}, bf16[1024,256]{1,0:T(8,128)(2,1)S(1)}, u32[]{:S(2)}, u32[]{:S(2)}) collective-permute-start(bf16[1024,256]{1,0:T(8,128)(2,1)} %sum_chunks.3.refs_0_), channel_id=1, source_target_pairs={{0,96},{1,97},{2,98},{3,99},{4,100},{5,101},{6,102},{7,103},{8,104... | collective-permute-start | bytes 1572872 | tf_op jit(solution)/shard_map/ppermute | solution.py:37
  95.3 23.7 %collective-permute-start.11 = (bf16[1024,256]{1,0:T(8,128)(2,1)}, bf16[1024,256]{1,0:T(8,128)(2,1)S(1)}, u32[]{:S(2)}, u32[]{:S(2)}) collective-permute-start(bf16[1024,256]{1,0:T(8,128)(2,1)} %sum_chunks.3.refs_0_), channel_id=1, source_target_pairs={{0,64},{1,65},{2,66},{3,67},{4,68},{5,69},{6,70},{7,71},{8,72},{9,... | collective-permute-start | bytes 1572872 | tf_op jit(solution)/shard_map/ppermute | solution.py:37
  95.8 24.6 %collective-permute-start.12 = (bf16[1024,256]{1,0:T(8,128)(2,1)}, bf16[1024,256]{1,0:T(8,128)(2,1)}, u32[]{:S(2)}, u32[]{:S(2)}) collective-permute-start(bf16[1024,256]{1,0:T(8,128)(2,1)} %sum_chunks.3.refs_0_), channel_id=1, source_target_pairs={{0,32},{1,33},{2,34},{3,35},{4,36},{5,37},{6,38},{7,39},{8,40},{9,... | collective-permute-start | bytes 1572872 | tf_op jit(solution)/shard_map/ppermute | solution.py:37
  96.4 28.0 %collective-permute-start.13 = (bf16[1024,256]{1,0:T(8,128)(2,1)}, bf16[1024,256]{1,0:T(8,128)(2,1)}, u32[]{:S(2)}, u32[]{:S(2)}) collective-permute-start(bf16[1024,256]{1,0:T(8,128)(2,1)} %sum_chunks.3.refs_0_), channel_id=1, source_target_pairs={{0,16},{1,17},{2,18},{3,19},{4,20},{5,21},{6,22},{7,23},{8,24},{9,... | collective-permute-start | bytes 1572872 | tf_op jit(solution)/shard_map/ppermute | solution.py:37
  112.9 8.5 %copy-start.2 = (bf16[1024,256]{1,0:T(8,128)(2,1)S(1)}, bf16[1024,256]{1,0:T(8,128)(2,1)}, u32[]{:S(2)}) copy-start(bf16[1024,256]{1,0:T(8,128)(2,1)} %sum_chunks.3.refs_0_) | copy-start | bytes 1572868
  120.4 4.0 %collective-permute-start.14 = (bf16[1024,256]{1,0:T(8,128)(2,1)S(1)}, bf16[1024,256]{1,0:T(8,128)(2,1)S(1)}, u32[]{:S(2)}, u32[]{:S(2)}) collective-permute-start(bf16[1024,256]{1,0:T(8,128)(2,1)S(1)} %collective-permute-done.10.refs_1_), channel_id=1, source_target_pairs={{0,16},{1,17},{2,18},{3,19},{4,20},{5,21},{6,22},{7,23},{8,24},{9,... | collective-permute-start | bytes 1572872 | tf_op jit(solution)/shard_map/ppermute | solution.py:37
  120.8 3.6 %collective-permute-start.15 = (bf16[1024,256]{1,0:T(8,128)(2,1)S(1)}, bf16[1024,256]{1,0:T(8,128)(2,1)S(1)}, u32[]{:S(2)}, u32[]{:S(2)}) collective-permute-start(bf16[1024,256]{1,0:T(8,128)(2,1)S(1)} %collective-permute-done.11.refs_2_), channel_id=1, source_target_pairs={{0,16},{1,17},{2,18},{3,19},{4,20},{5,21},{6,22},{7,23},{8,24},{9,... | collective-permute-start | bytes 1572872 | tf_op jit(solution)/shard_map/ppermute | solution.py:37
  120.9 3.5 %collective-permute-start.16 = (bf16[1024,256]{1,0:T(8,128)(2,1)}, bf16[1024,256]{1,0:T(8,128)(2,1)S(1)}, u32[]{:S(2)}, u32[]{:S(2)}) collective-permute-start(bf16[1024,256]{1,0:T(8,128)(2,1)} %collective-permute-done.12.refs_3_), channel_id=1, source_target_pairs={{0,16},{1,17},{2,18},{3,19},{4,20},{5,21},{6,22},{7,23},{8,24},{9,... | collective-permute-start | bytes 1572872 | tf_op jit(solution)/shard_map/ppermute | solution.py:37

commit v4 on v3

--- a/solution.py
+++ b/solution.py
@@ -226,8 +226,12 @@
     nv_ref, nm_ref, ns_ref = refs[-3:]
     arrived = refs[: len(refs) - (6 if len(refs) < 9 else 9)]
     base = pl.program_id(0) * rows
-    place = lax.broadcasted_iota(jnp.int32, (rows, slots), 0) + base
-    selector = jnp.where(index_ref[...] == place, 1.0, 0.0).astype(BF)
+    place = lax.broadcasted_iota(jnp.int32, (rows, 128), 0).astype(F32).astype(BF)
+    slot = (index_ref[...] - base).astype(F32).astype(BF)
+    one, zero = jnp.ones((rows, 128), BF), jnp.zeros((rows, 128), BF)
+    selector = jnp.concatenate(
+        [jnp.where(slot[:, k : k + 128] == place, one, zero) for k in range(0, slots, 128)], axis=1
+    )
     grad = [jnp.dot(selector, a[...], preferred_element_type=F32) for a in arrived]
     grad = grad[0] if len(grad) == 1 else jnp.concatenate(grad, axis=1)
     steps = steps_ref[0].astype(F32)

time: 128 us -> 128 us (level)
  no operation moved by 1% of the time
where the time goes in v4:
time: 128 us; the launch traced here: 127 us
  starting transfers between devices  43.5 us (34%)
  waiting for transfers between devices  41.5 us (32%)
  Pallas kernels  37.6 us (29%)
  local copies, waits for them, and re-layouts  2.41 us (2%)
  other arithmetic  1.52 us (1%)
    ppermute x17, starting transfers between devices, send(): return lax.ppermute(value, AXES, pairs)  29.2 us
    ppermute x17, waiting for transfers between devices, send(): return lax.ppermute(value, AXES, pairs)  26.2 us
    all_to_all x2, waiting for transfers between devices, exchange(): lax.all_to_all(ordered, AXES, split_axis=0, concat_axis=0, tiled=True)  15.3 us
    all_to_all x2, starting transfers between devices, exchange(): lax.all_to_all(ordered, AXES, split_axis=0, concat_axis=0, tiled=True)  14.3 us
    pallas_call x2, Pallas kernels, adam(): pl.pallas_call(adam_kernel, grid=(owned // rows,), in_specs=[pl.BlockSpec...  12.8 us
    pallas_call x2, Pallas kernels, place_half(): pl.pallas_call(place_kernel, in_specs=[pl.BlockSpec(memory_space=pltpu.SM...  5.85 us
    pallas_call x1, Pallas kernels, partials(): pl.pallas_call(partials_kernel, grid_spec=pltpu.PrefetchScalarGridSpec(nu...  5.53 us
    pallas_call x2, Pallas kernels, sum_chunks(): pl.pallas_call(sum_kernel, out_shape=pltpu.HBM(chunks[0].shape, BF), cost...  4.81 us
  transfers between devices with their start and end apart: 19, of which 7 were waited for; matrix products, arithmetic and copies ran while one was open for 1% of the time, Pallas kernels for 22%

profile of v4, /device:TPU:1, one launch (start us, length us, event | category | flops | bytes accessed | tf_op | source)
XLA Modules:
  0.0 127.4 jit_solution(7985828329055593642)
XLA Ops:
  0.8 2.2 %copy-done.1 = bf16[256,2,4096]{2,1,0:T(2,128)(2,1)S(1)} copy-done((bf16[256,2,4096]{2,1,0:T(2,128)(2,1)S(1)}, bf16[256,2,4096]{2,1,0:T(2,128)(2,1)}, u32[]{:S(2)}) %copy-start.1) | copy-done | bytes 4194328
  2.9 5.5 %partials.1 = (bf16[4,1024,256]{2,1,0:T(8,128)(2,1)S(1)}, bf16[4,1024,256]{2,1,0:T(8,128)(2,1)S(1)}) custom-call(s32[4]{0:T(128)S(1)} %pad_add_fusion.place_ref, bf16[256,2,4096]{2,1,0:T(2,128)(2,1)S(1)} %copy-done.1, bf16[256,2,256]{2,1,0:T(2,128)(2,1)} %query_ref.1), custom_call_target="tpu_custom_call" | custom-call | tf_op jit(solution)/shard_map/partials/pallas_call | solution.py:129
  8.5 1.5 %collective-permute-start = (bf16[4,1024,256]{2,1,0:T(8,128)(2,1)S(1)}, bf16[4,1024,256]{2,1,0:T(8,128)(2,1)S(1)}, u32[]{:S(2)}, u32[]{:S(2)}) collective-permute-start(bf16[4,1024,256]{2,1,0:T(8,128)(2,1)S(1)} %get-tuple-element.38), channel_id=1, source_target_pairs={{0,16},{1,17},{2,18},{3,19},{4,20},{5,21},{6,22},{7,23},{8,24},{9,... | collective-permute-start | bytes 6291464 | tf_op jit(solution)/shard_map/ppermute | solution.py:37
  10.0 4.6 %combine_first.1 = (bf16[128,32,256]{2,1,0:T(8,128)(2,1)}, bf16[512,256]{1,0:T(8,128)(2,1)}) custom-call(s32[32,256]{1,0:T(8,128)S(1)} %bitcast.10, f32[32,256]{1,0:T(8,128)S(1)} %bitcast.11, bf16[256,4096]{1,0:T(8,128)(2,1)S(1)} %copy-done, bf16[256,4096]{1,0:T(8,128)(2,1)S(1)} %copy-done), custom_call_target="tpu_custom_call" | custom-call | tf_op jit(solution)/shard_map/combine_first/pallas_call | solution.py:91
  14.6 1.4 %merge.1 = (bf16[1024,256]{1,0:T(8,128)(2,1)S(1)}, bf16[1024,256]{1,0:T(8,128)(2,1)}, bf16[1024,256]{1,0:T(8,128)(2,1)}, bf16[1024,256]{1,0:T(8,128)(2,1)S(1)}) custom-call(bf16[4,1024,256]{2,1,0:T(8,128)(2,1)S(1)} %get-tuple-element.37.own_ref, bf16[4,1024,256]{2,1,0:T(8,128)(2,1)S(1)} %collective-permute-done.got_ref), custom_call_target="tpu_custom_call" | custom-call | tf_op jit(solution)/shard_map/merge/pallas_call | solution.py:155
  15.9 1.4 %collective-permute-start.1 = (bf16[1024,256]{1,0:T(8,128)(2,1)}, bf16[1024,256]{1,0:T(8,128)(2,1)}, u32[]{:S(2)}, u32[]{:S(2)}) collective-permute-start(bf16[1024,256]{1,0:T(8,128)(2,1)} %get-tuple-element.44), channel_id=1, source_target_pairs={{0,32},{1,33},{2,34},{3,35},{4,36},{5,37},{6,38},{7,39},{8,40},{9,... | collective-permute-start | bytes 1572872 | tf_op jit(solution)/shard_map/ppermute | solution.py:37
  17.3 2.6 %collective-permute-start.2 = (bf16[1024,256]{1,0:T(8,128)(2,1)}, bf16[1024,256]{1,0:T(8,128)(2,1)}, u32[]{:S(2)}, u32[]{:S(2)}) collective-permute-start(bf16[1024,256]{1,0:T(8,128)(2,1)} %get-tuple-element.45), channel_id=1, source_target_pairs={{0,64},{1,65},{2,66},{3,67},{4,68},{5,69},{6,70},{7,71},{8,72},{9,... | collective-permute-start | bytes 1572872 | tf_op jit(solution)/shard_map/ppermute | solution.py:37
  19.9 1.1 collective-permute-start.3
  21.0 8.7 %all-to-all-start = ((bf16[128,32,256]{2,1,0:T(8,128)(2,1)}), bf16[128,32,256]{2,1,0:T(8,128)(2,1)}, u32[]{:S(2)}, u32[]{:S(2)}) async-start(bf16[128,32,256]{2,1,0:T(8,128)(2,1)} %get-tuple-element.47), calls=%async_computation | async-start | bytes 4194304 | tf_op jit(solution)/shard_map/all_to_all | solution.py:318
  29.8 3.0 %collective-permute-done.2.c_ref = bf16[1024,256]{1,0:T(8,128)(2,1)} collective-permute-done((bf16[1024,256]{1,0:T(8,128)(2,1)}, bf16[1024,256]{1,0:T(8,128)(2,1)}, u32[]{:S(2)}, u32[]{:S(2)}) %collective-permute-start.2) | collective-permute-done | bytes 524320 | tf_op jit(solution)/shard_map/ppermute | solution.py:37
  33.4 2.4 %sum_chunks.2 = bf16[1024,256]{1,0:T(8,128)(2,1)} custom-call(bf16[1024,256]{1,0:T(8,128)(2,1)S(1)} %get-tuple-element.43.a_ref, bf16[1024,256]{1,0:T(8,128)(2,1)} %collective-permute-done.1.b_ref, bf16[1024,256]{1,0:T(8,128)(2,1)} %collective-permute-done.2.c_ref, bf16[1024,256]{1,0:T(8,128)(2,1)} %collective-permute-done.3.d_ref), custom_call_target="tpu_custom_call" | custom-call | flops 99999997952 | tf_op jit(solution)/shard_map/sum_chunks/pallas_call | solution.py:170
  35.8 8.0 %collective-permute-start.6 = (bf16[1024,256]{1,0:T(8,128)(2,1)}, bf16[1024,256]{1,0:T(8,128)(2,1)S(1)}, u32[]{:S(2)}, u32[]{:S(2)}) collective-permute-start(bf16[1024,256]{1,0:T(8,128)(2,1)} %sum_chunks.2), channel_id=1, source_target_pairs={{0,12},{1,13},{2,14},{3,15},{4,0},{5,1},{6,2},{7,3},{8,4},{9,5},{1... | collective-permute-start | bytes 1572872 | tf_op jit(solution)/shard_map/ppermute | solution.py:37
  43.8 2.1 %collective-permute-start.5 = (bf16[1024,256]{1,0:T(8,128)(2,1)}, bf16[1024,256]{1,0:T(8,128)(2,1)S(1)}, u32[]{:S(2)}, u32[]{:S(2)}) collective-permute-start(bf16[1024,256]{1,0:T(8,128)(2,1)} %sum_chunks.2), channel_id=1, source_target_pairs={{0,4},{1,5},{2,6},{3,7},{4,8},{5,9},{6,10},{7,11},{8,12},{9,13},{1... | collective-permute-start | bytes 1572872 | tf_op jit(solution)/shard_map/ppermute | solution.py:37
  45.9 1.7 %collective-permute-start.4 = (bf16[1024,256]{1,0:T(8,128)(2,1)}, bf16[1024,256]{1,0:T(8,128)(2,1)S(1)}, u32[]{:S(2)}, u32[]{:S(2)}) collective-permute-start(bf16[1024,256]{1,0:T(8,128)(2,1)} %sum_chunks.2), channel_id=1, source_target_pairs={{0,8},{1,9},{2,10},{3,11},{4,12},{5,13},{6,14},{7,15},{8,0},{9,1},... | collective-permute-start | bytes 1572872 | tf_op jit(solution)/shard_map/ppermute | solution.py:37
  47.6 13.9 %collective-permute-done.6 = bf16[1024,256]{1,0:T(8,128)(2,1)S(1)} collective-permute-done((bf16[1024,256]{1,0:T(8,128)(2,1)}, bf16[1024,256]{1,0:T(8,128)(2,1)S(1)}, u32[]{:S(2)}, u32[]{:S(2)}) %collective-permute-start.6) | collective-permute-done | bytes 524320 | tf_op jit(solution)/shard_map/ppermute | solution.py:37
  61.5 1.5 %collective-permute-done.5 = bf16[1024,256]{1,0:T(8,128)(2,1)S(1)} collective-permute-done((bf16[1024,256]{1,0:T(8,128)(2,1)}, bf16[1024,256]{1,0:T(8,128)(2,1)S(1)}, u32[]{:S(2)}, u32[]{:S(2)}) %collective-permute-start.5) | collective-permute-done | bytes 524320 | tf_op jit(solution)/shard_map/ppermute | solution.py:37
  63.0 5.6 %collective-permute-done.4 = bf16[1024,256]{1,0:T(8,128)(2,1)S(1)} collective-permute-done((bf16[1024,256]{1,0:T(8,128)(2,1)}, bf16[1024,256]{1,0:T(8,128)(2,1)S(1)}, u32[]{:S(2)}, u32[]{:S(2)}) %collective-permute-start.4) | collective-permute-done | bytes 524320 | tf_op jit(solution)/shard_map/ppermute | solution.py:37
  68.6 1.3 %add_convert_fusion.a_ref.after_ref = bf16[1024,256]{1,0:T(8,128)(2,1)S(1)} fusion(bf16[1024,256]{1,0:T(8,128)(2,1)S(1)} %collective-permute-done.6, bf16[1024,256]{1,0:T(8,128)(2,1)S(1)} %collective-permute-done.5, bf16[1024,256]{1,0:T(8,128)(2,1)S(1)} %collective-permute-done.4, bf16[1024,256]{1,0:T(8,128)(2,1)} %sum_chunks.2), kind=kLoop, calls=%fused_computation | loop fusion | flops 2097152 | bytes 2621440 | tf_op jit(solution)/shard_map/convert_element_type | solution.py:181
  69.9 1.2 collective-permute-start.7
  71.1 3.0 %collective-permute-start.8 = (bf16[1024,256]{1,0:T(8,128)(2,1)S(1)}, bf16[1024,256]{1,0:T(8,128)(2,1)}, u32[]{:S(2)}, u32[]{:S(2)}) collective-permute-start(bf16[1024,256]{1,0:T(8,128)(2,1)S(1)} %add_convert_fusion.a_ref.after_ref), channel_id=1, source_target_pairs={{0,2},{1,3},{2,0},{3,1},{4,6},{5,7},{6,4},{7,5},{8,10},{9,11},{10,... | collective-permute-start | bytes 1572872 | tf_op jit(solution)/shard_map/ppermute | solution.py:37
  74.1 0.8 collective-permute-start.9
  75.1 2.6 %combine_next.1 = bf16[128,32,256]{2,1,0:T(8,128)(2,1)} custom-call(bf16[1024,256]{1,0:T(8,128)(2,1)S(1)} %add_convert_fusion.a_ref.after_ref, bf16[512,256]{1,0:T(8,128)(2,1)S(1)} %copy-done.3, bf16[256,4096]{1,0:T(8,128)(2,1)S(1)} %copy-done, bf16[256,4096]{1,0:T(8,128)(2,1)S(1)} %copy-done), custom_call_target="tpu_custom_call" | custom-call | tf_op jit(solution)/shard_map/combine_next/pallas_call | solution.py:100
  77.8 5.6 %all-to-all-start.1 = ((bf16[128,32,256]{2,1,0:T(8,128)(2,1)}), bf16[128,32,256]{2,1,0:T(8,128)(2,1)S(1)}, u32[]{:S(2)}, u32[]{:S(2)}) async-start(bf16[128,32,256]{2,1,0:T(8,128)(2,1)} %combine_next.1), calls=%async_computation.1 | async-start | bytes 4194304 | tf_op jit(solution)/shard_map/all_to_all | solution.py:318
  83.4 6.8 %adam.2 = (f32[1024,512]{1,0:T(8,128)}, f32[1024,512]{1,0:T(8,128)}, f32[1024,512]{1,0:T(8,128)}) custom-call(s32[1,4096]{1,0:T(1,128)S(1)} %reshape.20.index_ref, s32[4,1,256]{2,1,0:T(1,128)S(1)} %bitcast.12, bf16[4096,256]{1,0:T(8,128)(2,1)} %bitcast.7.refs_0_, f32[1024,512]{1,0:T(8,128)} %refs_1_.3, f32[1024,512]{1,0:T(8,128)} %refs_2_.3, f32[1024,512]{1,0:T(8,128)} %refs_3_.3), custom_call_target="tpu_custom_call" | custom-call | tf_op jit(solution)/shard_map/adam/pallas_call | solution.py:257
  90.2 2.4 %sum_chunks.3.refs_0_ = bf16[1024,256]{1,0:T(8,128)(2,1)} custom-call(bf16[1024,256]{1,0:T(8,128)(2,1)S(1)} %add_convert_fusion.a_ref.after_ref, bf16[1024,256]{1,0:T(8,128)(2,1)} %collective-permute-done.7.b_ref, bf16[1024,256]{1,0:T(8,128)(2,1)} %collective-permute-done.8.c_ref, bf16[1024,256]{1,0:T(8,128)(2,1)} %collective-permute-done.9.d_ref), custom_call_target="tpu_custom_call" | custom-call | flops 99999997952 | tf_op jit(solution)/shard_map/sum_chunks/pallas_call | solution.py:170
  92.6 2.7 %collective-permute-start.10 = (bf16[1024,256]{1,0:T(8,128)(2,1)}, bf16[1024,256]{1,0:T(8,128)(2,1)S(1)}, u32[]{:S(2)}, u32[]{:S(2)}) collective-permute-start(bf16[1024,256]{1,0:T(8,128)(2,1)} %sum_chunks.3.refs_0_), channel_id=1, source_target_pairs={{0,96},{1,97},{2,98},{3,99},{4,100},{5,101},{6,102},{7,103},{8,104... | collective-permute-start | bytes 1572872 | tf_op jit(solution)/shard_map/ppermute | solution.py:37
  96.4 1.2 collective-permute-start.13
  97.6 15.3 %all-to-all-done.1 = bf16[128,32,256]{2,1,0:T(8,128)(2,1)S(1)} async-done(((bf16[128,32,256]{2,1,0:T(8,128)(2,1)}), bf16[128,32,256]{2,1,0:T(8,128)(2,1)S(1)}, u32[]{:S(2)}, u32[]{:S(2)}) %all-to-all-start.1) | async-done | bytes 2097184 | tf_op jit(solution)/shard_map/all_to_all | solution.py:318
  112.9 6.0 %adam.3 = (f32[1024,512]{1,0:T(8,128)}, f32[1024,512]{1,0:T(8,128)}, f32[1024,512]{1,0:T(8,128)}) custom-call(s32[1,4096]{1,0:T(1,128)S(1)} %reshape.20.index_ref, s32[4,1,256]{2,1,0:T(1,128)S(1)} %bitcast.13, bf16[4096,256]{1,0:T(8,128)(2,1)S(1)} %bitcast.9, f32[1024,512]{1,0:T(8,128)} %refs_1_.3, ...), custom_call_target="tpu_custom_call", output_to_operand_aliasing={{0}: (6, {}), {1}: (7, {}), {2}: (8, {})} | custom-call | tf_op jit(solution)/shard_map/adam/pallas_call | solution.py:257
  119.0 1.4 %collective-permute-done.12.refs_3_ = bf16[1024,256]{1,0:T(8,128)(2,1)} collective-permute-done((bf16[1024,256]{1,0:T(8,128)(2,1)}, bf16[1024,256]{1,0:T(8,128)(2,1)}, u32[]{:S(2)}, u32[]{:S(2)}) %collective-permute-start.12) | collective-permute-done | bytes 524320 | tf_op jit(solution)/shard_map/ppermute | solution.py:37
  121.5 2.9 %place_half.2.refs_4_ = bf16[2,4096,256]{2,1,0:T(8,128)(2,1)} custom-call(s32[2]{0:T(128)S(1)} %pad_add_fusion.2.place_ref, bf16[1024,256]{1,0:T(8,128)(2,1)S(1)} %copy-done.2, bf16[1024,256]{1,0:T(8,128)(2,1)S(1)} %collective-permute-done.10.refs_1_, bf16[1024,256]{1,0:T(8,128)(2,1)S(1)} %collective-permute-done.11.refs_2_, ...), custom_call_target="tpu_custom_call" | custom-call | tf_op jit(solution)/shard_map/place_half/pallas_call | solution.py:205
  124.4 3.0 %place_half.3 = bf16[2,4096,256]{2,1,0:T(8,128)(2,1)} custom-call(s32[2]{0:T(128)S(1)} %pad_add_fusion.1.place_ref, bf16[1024,256]{1,0:T(8,128)(2,1)} %collective-permute-done.13.refs_0_, bf16[1024,256]{1,0:T(8,128)(2,1)S(1)} %collective-permute-done.14.refs_1_, ...), custom_call_target="tpu_custom_call", output_to_operand_aliasing={{}: (5, {})} | custom-call | tf_op jit(solution)/shard_map/place_half/pallas_call | solution.py:205
  (38 shorter events, 3.2 us)
Async XLA Ops:
  0.7 2.2 %copy-start.1 = (bf16[256,2,4096]{2,1,0:T(2,128)(2,1)S(1)}, bf16[256,2,4096]{2,1,0:T(2,128)(2,1)}, u32[]{:S(2)}) copy-start(bf16[256,2,4096]{2,1,0:T(2,128)(2,1)} %score_ref.1) | copy-start | bytes 12582916
  2.9 7.0 %copy-start = (bf16[256,4096]{1,0:T(8,128)(2,1)S(1)}, bf16[256,4096]{1,0:T(8,128)(2,1)}, u32[]{:S(2)}) copy-start(bf16[256,4096]{1,0:T(8,128)(2,1)} %high_ref.3) | copy-start | bytes 6291460
  2.9 7.0 %copy-start.4 = (s32[256,32]{0,1:T(8,128)S(1)}, s32[256,32]{0,1:T(8,128)}, u32[]{:S(2)}) copy-start(s32[256,32]{0,1:T(8,128)} %param.12) | copy-start | bytes 98308
  2.9 7.0 %copy-start.5 = (f32[256,32]{0,1:T(8,128)S(1)}, f32[256,32]{0,1:T(8,128)}, u32[]{:S(2)}) copy-start(f32[256,32]{0,1:T(8,128)} %param.11) | copy-start | bytes 98308
  8.5 6.1 %collective-permute-start = (bf16[4,1024,256]{2,1,0:T(8,128)(2,1)S(1)}, bf16[4,1024,256]{2,1,0:T(8,128)(2,1)S(1)}, u32[]{:S(2)}, u32[]{:S(2)}) collective-permute-start(bf16[4,1024,256]{2,1,0:T(8,128)(2,1)S(1)} %get-tuple-element.38), channel_id=1, source_target_pairs={{0,16},{1,17},{2,18},{3,19},{4,20},{5,21},{6,22},{7,23},{8,24},{9,... | collective-permute-start | bytes 6291464 | tf_op jit(solution)/shard_map/ppermute | solution.py:37
  15.9 13.8 %collective-permute-start.1 = (bf16[1024,256]{1,0:T(8,128)(2,1)}, bf16[1024,256]{1,0:T(8,128)(2,1)}, u32[]{:S(2)}, u32[]{:S(2)}) collective-permute-start(bf16[1024,256]{1,0:T(8,128)(2,1)} %get-tuple-element.44), channel_id=1, source_target_pairs={{0,32},{1,33},{2,34},{3,35},{4,36},{5,37},{6,38},{7,39},{8,40},{9,... | collective-permute-start | bytes 1572872 | tf_op jit(solution)/shard_map/ppermute | solution.py:37
  17.3 15.4 %collective-permute-start.2 = (bf16[1024,256]{1,0:T(8,128)(2,1)}, bf16[1024,256]{1,0:T(8,128)(2,1)}, u32[]{:S(2)}, u32[]{:S(2)}) collective-permute-start(bf16[1024,256]{1,0:T(8,128)(2,1)} %get-tuple-element.45), channel_id=1, source_target_pairs={{0,64},{1,65},{2,66},{3,67},{4,68},{5,69},{6,70},{7,71},{8,72},{9,... | collective-permute-start | bytes 1572872 | tf_op jit(solution)/shard_map/ppermute | solution.py:37
  19.9 13.5 %collective-permute-start.3 = (bf16[1024,256]{1,0:T(8,128)(2,1)S(1)}, bf16[1024,256]{1,0:T(8,128)(2,1)}, u32[]{:S(2)}, u32[]{:S(2)}) collective-permute-start(bf16[1024,256]{1,0:T(8,128)(2,1)S(1)} %get-tuple-element.46), channel_id=1, source_target_pairs={{0,96},{1,97},{2,98},{3,99},{4,100},{5,101},{6,102},{7,103},{8,104... | collective-permute-start | bytes 1572872 | tf_op jit(solution)/shard_map/ppermute | solution.py:37
  21.0 56.8 %all-to-all-start = ((bf16[128,32,256]{2,1,0:T(8,128)(2,1)}), bf16[128,32,256]{2,1,0:T(8,128)(2,1)}, u32[]{:S(2)}, u32[]{:S(2)}) async-start(bf16[128,32,256]{2,1,0:T(8,128)(2,1)} %get-tuple-element.47), calls=%async_computation | async-start | bytes 4194304 | tf_op jit(solution)/shard_map/all_to_all | solution.py:318
  35.8 39.1 %copy-start.7 = (s32[1,128,32]{1,2,0:T(8,128)S(1)}, s32[1,128,32]{1,2,0:T(8,128)}, u32[]{:S(2)}) copy-start(s32[1,128,32]{1,2,0:T(8,128)} %param.13) | copy-start | bytes 49156
  35.8 39.3 %copy-start.3 = (bf16[512,256]{1,0:T(8,128)(2,1)S(1)}, bf16[512,256]{1,0:T(8,128)(2,1)}, u32[]{:S(2)}) copy-start(bf16[512,256]{1,0:T(8,128)(2,1)} %get-tuple-element.55.mix_ref) | copy-start | bytes 786436
  35.8 25.7 %collective-permute-start.6 = (bf16[1024,256]{1,0:T(8,128)(2,1)}, bf16[1024,256]{1,0:T(8,128)(2,1)S(1)}, u32[]{:S(2)}, u32[]{:S(2)}) collective-permute-start(bf16[1024,256]{1,0:T(8,128)(2,1)} %sum_chunks.2), channel_id=1, source_target_pairs={{0,12},{1,13},{2,14},{3,15},{4,0},{5,1},{6,2},{7,3},{8,4},{9,5},{1... | collective-permute-start | bytes 1572872 | tf_op jit(solution)/shard_map/ppermute | solution.py:37
  43.8 19.2 %collective-permute-start.5 = (bf16[1024,256]{1,0:T(8,128)(2,1)}, bf16[1024,256]{1,0:T(8,128)(2,1)S(1)}, u32[]{:S(2)}, u32[]{:S(2)}) collective-permute-start(bf16[1024,256]{1,0:T(8,128)(2,1)} %sum_chunks.2), channel_id=1, source_target_pairs={{0,4},{1,5},{2,6},{3,7},{4,8},{5,9},{6,10},{7,11},{8,12},{9,13},{1... | collective-permute-start | bytes 1572872 | tf_op jit(solution)/shard_map/ppermute | solution.py:37
  45.9 22.8 %collective-permute-start.4 = (bf16[1024,256]{1,0:T(8,128)(2,1)}, bf16[1024,256]{1,0:T(8,128)(2,1)S(1)}, u32[]{:S(2)}, u32[]{:S(2)}) collective-permute-start(bf16[1024,256]{1,0:T(8,128)(2,1)} %sum_chunks.2), channel_id=1, source_target_pairs={{0,8},{1,9},{2,10},{3,11},{4,12},{5,13},{6,14},{7,15},{8,0},{9,1},... | collective-permute-start | bytes 1572872 | tf_op jit(solution)/shard_map/ppermute | solution.py:37
  69.9 20.3 %collective-permute-start.7 = (bf16[1024,256]{1,0:T(8,128)(2,1)S(1)}, bf16[1024,256]{1,0:T(8,128)(2,1)}, u32[]{:S(2)}, u32[]{:S(2)}) collective-permute-start(bf16[1024,256]{1,0:T(8,128)(2,1)S(1)} %add_convert_fusion.a_ref.after_ref), channel_id=1, source_target_pairs={{0,1},{1,2},{2,3},{3,0},{4,5},{5,6},{6,7},{7,4},{8,9},{9,10},{10,1... | collective-permute-start | bytes 1572872 | tf_op jit(solution)/shard_map/ppermute | solution.py:37
  71.1 19.1 %collective-permute-start.8 = (bf16[1024,256]{1,0:T(8,128)(2,1)S(1)}, bf16[1024,256]{1,0:T(8,128)(2,1)}, u32[]{:S(2)}, u32[]{:S(2)}) collective-permute-start(bf16[1024,256]{1,0:T(8,128)(2,1)S(1)} %add_convert_fusion.a_ref.after_ref), channel_id=1, source_target_pairs={{0,2},{1,3},{2,0},{3,1},{4,6},{5,7},{6,4},{7,5},{8,10},{9,11},{10,... | collective-permute-start | bytes 1572872 | tf_op jit(solution)/shard_map/ppermute | solution.py:37
  74.1 16.1 %collective-permute-start.9 = (bf16[1024,256]{1,0:T(8,128)(2,1)S(1)}, bf16[1024,256]{1,0:T(8,128)(2,1)}, u32[]{:S(2)}, u32[]{:S(2)}) collective-permute-start(bf16[1024,256]{1,0:T(8,128)(2,1)S(1)} %add_convert_fusion.a_ref.after_ref), channel_id=1, source_target_pairs={{0,3},{1,0},{2,1},{3,2},{4,7},{5,4},{6,5},{7,6},{8,11},{9,8},{10,9... | collective-permute-start | bytes 1572872 | tf_op jit(solution)/shard_map/ppermute | solution.py:37
  77.8 5.6 %copy-start.6 = (s32[1024]{0:T(1024)S(1)}, s32[1024]{0:T(1024)}, u32[]{:S(2)}) copy-start(s32[1024]{0:T(1024)} %param.17) | copy-start | bytes 12292
  77.8 35.2 %all-to-all-start.1 = ((bf16[128,32,256]{2,1,0:T(8,128)(2,1)}), bf16[128,32,256]{2,1,0:T(8,128)(2,1)S(1)}, u32[]{:S(2)}, u32[]{:S(2)}) async-start(bf16[128,32,256]{2,1,0:T(8,128)(2,1)} %combine_next.1), calls=%async_computation.1 | async-start | bytes 4194304 | tf_op jit(solution)/shard_map/all_to_all | solution.py:318
  92.6 26.3 %collective-permute-start.10 = (bf16[1024,256]{1,0:T(8,128)(2,1)}, bf16[1024,256]{1,0:T(8,128)(2,1)S(1)}, u32[]{:S(2)}, u32[]{:S(2)}) collective-permute-start(bf16[1024,256]{1,0:T(8,128)(2,1)} %sum_chunks.3.refs_0_), channel_id=1, source_target_pairs={{0,96},{1,97},{2,98},{3,99},{4,100},{5,101},{6,102},{7,103},{8,104... | collective-permute-start | bytes 1572872 | tf_op jit(solution)/shard_map/ppermute | solution.py:37
  95.3 23.7 %collective-permute-start.11 = (bf16[1024,256]{1,0:T(8,128)(2,1)}, bf16[1024,256]{1,0:T(8,128)(2,1)S(1)}, u32[]{:S(2)}, u32[]{:S(2)}) collective-permute-start(bf16[1024,256]{1,0:T(8,128)(2,1)} %sum_chunks.3.refs_0_), channel_id=1, source_target_pairs={{0,64},{1,65},{2,66},{3,67},{4,68},{5,69},{6,70},{7,71},{8,72},{9,... | collective-permute-start | bytes 1572872 | tf_op jit(solution)/shard_map/ppermute | solution.py:37
  95.8 24.6 %collective-permute-start.12 = (bf16[1024,256]{1,0:T(8,128)(2,1)}, bf16[1024,256]{1,0:T(8,128)(2,1)}, u32[]{:S(2)}, u32[]{:S(2)}) collective-permute-start(bf16[1024,256]{1,0:T(8,128)(2,1)} %sum_chunks.3.refs_0_), channel_id=1, source_target_pairs={{0,32},{1,33},{2,34},{3,35},{4,36},{5,37},{6,38},{7,39},{8,40},{9,... | collective-permute-start | bytes 1572872 | tf_op jit(solution)/shard_map/ppermute | solution.py:37
  96.4 28.0 %collective-permute-start.13 = (bf16[1024,256]{1,0:T(8,128)(2,1)}, bf16[1024,256]{1,0:T(8,128)(2,1)}, u32[]{:S(2)}, u32[]{:S(2)}) collective-permute-start(bf16[1024,256]{1,0:T(8,128)(2,1)} %sum_chunks.3.refs_0_), channel_id=1, source_target_pairs={{0,16},{1,17},{2,18},{3,19},{4,20},{5,21},{6,22},{7,23},{8,24},{9,... | collective-permute-start | bytes 1572872 | tf_op jit(solution)/shard_map/ppermute | solution.py:37
  112.9 8.5 %copy-start.2 = (bf16[1024,256]{1,0:T(8,128)(2,1)S(1)}, bf16[1024,256]{1,0:T(8,128)(2,1)}, u32[]{:S(2)}) copy-start(bf16[1024,256]{1,0:T(8,128)(2,1)} %sum_chunks.3.refs_0_) | copy-start | bytes 1572868
  120.4 4.0 %collective-permute-start.14 = (bf16[1024,256]{1,0:T(8,128)(2,1)S(1)}, bf16[1024,256]{1,0:T(8,128)(2,1)S(1)}, u32[]{:S(2)}, u32[]{:S(2)}) collective-permute-start(bf16[1024,256]{1,0:T(8,128)(2,1)S(1)} %collective-permute-done.10.refs_1_), channel_id=1, source_target_pairs={{0,16},{1,17},{2,18},{3,19},{4,20},{5,21},{6,22},{7,23},{8,24},{9,... | collective-permute-start | bytes 1572872 | tf_op jit(solution)/shard_map/ppermute | solution.py:37
  120.8 3.6 %collective-permute-start.15 = (bf16[1024,256]{1,0:T(8,128)(2,1)S(1)}, bf16[1024,256]{1,0:T(8,128)(2,1)S(1)}, u32[]{:S(2)}, u32[]{:S(2)}) collective-permute-start(bf16[1024,256]{1,0:T(8,128)(2,1)S(1)} %collective-permute-done.11.refs_2_), channel_id=1, source_target_pairs={{0,16},{1,17},{2,18},{3,19},{4,20},{5,21},{6,22},{7,23},{8,24},{9,... | collective-permute-start | bytes 1572872 | tf_op jit(solution)/shard_map/ppermute | solution.py:37
  120.9 3.5 %collective-permute-start.16 = (bf16[1024,256]{1,0:T(8,128)(2,1)}, bf16[1024,256]{1,0:T(8,128)(2,1)S(1)}, u32[]{:S(2)}, u32[]{:S(2)}) collective-permute-start(bf16[1024,256]{1,0:T(8,128)(2,1)} %collective-permute-done.12.refs_3_), channel_id=1, source_target_pairs={{0,16},{1,17},{2,18},{3,19},{4,20},{5,21},{6,22},{7,23},{8,24},{9,... | collective-permute-start | bytes 1572872 | tf_op jit(solution)/shard_map/ppermute | solution.py:37
